TPU v7x, 128 devices: a whole 4x4x4 slice. The times are simulated.
128 devices in a mesh: gx: 4 (over x_lo, core), gy: 8 (over z, x_hi), gz: 4 (over y).
Axes of the slice: x: 4 (x_hi: 2, x_lo: 2; x = x_hi * 2 + x_lo), y: 4, z: 4, core: 2. Of those that a mesh axis runs over, the one named last changes fastest.
Arguments:
- inputs: bfloat16 [3072, 6144], P('gy', ('gz', 'gx')), may hold values from -6 to 6
- weight: bfloat16 [6144, 24576], P('gz', ('gx', 'gy')), may hold values from -0.078125 to 0.078125
- cotangent: bfloat16 [3072, 24576], P('gy', ('gx', 'gz')), may hold values from -3 to 3
Outputs:
- activation: bfloat16 [3072, 24576], P('gy', ('gx', 'gz'))
- input_grad: bfloat16 [3072, 6144], P('gy', ('gz', 'gx'))
- weight_grad: bfloat16 [6144, 24576], P('gz', ('gx', 'gy'))
All inputs are finite; a program needn't handle non-finite values.
Results may differ from a plain program's by a relative error of at most 0.02.
Values may be sent and summed in bfloat16 or wider, within the bound.
A program may use at most 192 MiB of HBM per device.

v0:
```python
import jax
import jax.numpy as jnp
from jax import lax
from jax.sharding import PartitionSpec as P


def gelu_tanh(value):
    return jax.nn.gelu(value, approximate=True)


def on_device(inputs, weight, cotangent):
    row_inputs = lax.all_gather(inputs, "gx", axis=1, tiled=True)
    weight_cols = lax.all_gather(weight, "gy", axis=1, tiled=True)
    partial_value = jnp.dot(row_inputs, weight_cols, preferred_element_type=jnp.float32)
    preact = lax.psum_scatter(
        partial_value.astype(jnp.bfloat16), "gz", scatter_dimension=1, tiled=True
    ).astype(jnp.float32)
    output, slope_fn = jax.vjp(gelu_tanh, preact)
    activation = output.astype(jnp.bfloat16)
    own_slopes = slope_fn(cotangent.astype(jnp.float32))[0].astype(jnp.bfloat16)
    slopes = lax.all_gather(own_slopes, "gz", axis=1, tiled=True)
    input_terms = lax.dot_general(
        slopes, weight_cols, (((1,), (1,)), ((), ())), preferred_element_type=jnp.float32
    )
    input_grad = lax.psum_scatter(
        input_terms.astype(jnp.bfloat16), "gx", scatter_dimension=1, tiled=True
    )
    weight_terms = lax.dot_general(
        row_inputs, slopes, (((0,), (0,)), ((), ())), preferred_element_type=jnp.float32
    )
    weight_grad = lax.psum_scatter(
        weight_terms.astype(jnp.bfloat16), "gy", scatter_dimension=1, tiled=True
    )
    return (activation, input_grad, weight_grad)


def solution(mesh):
    return jax.shard_map(
        on_device,
        mesh=mesh,
        in_specs=(P("gy", ("gz", "gx")), P("gz", ("gx", "gy")), P("gy", ("gx", "gz"))),
        out_specs=(P("gy", ("gx", "gz")), P("gy", ("gz", "gx")), P("gz", ("gx", "gy"))),
        check_vma=False,
    )
```

profile of v0, /device:TPU:1, one launch (start us, length us, event | category | flops | bytes accessed | tf_op | source)
XLA Modules:
  0.0 616.9 jit_solution(7992530026773539132)
XLA Ops:
  7.2 0.0 all-gather.4.cloned.1.call-start
  7.2 0.7 all-gather.4.cloned.1.call-update
  7.9 0.0 all-gather.6.cloned.1.call-start
  7.9 0.7 all-gather.6.cloned.1.call-update
  8.6 0.0 reduce-scatter.6.cloned.1.call-start
  8.7 26.2 %all-gather.4.cloned.1.call-done = bf16[384,1536]{1,0:T(8,128)(2,1)} async-done(((bf16[384,384]{1,0:T(8,128)(2,1)}), bf16[384,1536]{1,0:T(8,128)(2,1)}) %all-gather.4.cloned.1.call-update) | async-done | bytes 1179664 | tf_op jit(solution)/shard_map/all_gather | solution.py:12
  34.9 203.3 %all-gather.6.cloned.1.call-done = bf16[1536,6144]{1,0:T(8,128)(2,1)} async-done(((bf16[1536,768]{1,0:T(8,128)(2,1)}), bf16[1536,6144]{1,0:T(8,128)(2,1)}) %all-gather.6.cloned.1.call-update) | async-done | bytes 18874384 | tf_op jit(solution)/shard_map/all_gather | solution.py:13
  238.2 13.0 %convolution_convert_fusion.1 = bf16[384,6144]{1,0:T(8,128)(2,1)} fusion(bf16[384,1536]{1,0:T(8,128)(2,1)} %all-gather.4.cloned.1.call-done, bf16[1536,6144]{1,0:T(8,128)(2,1)} %all-gather.6.cloned.1.call-done), kind=kOutput, calls=%fused_computation.2 | convolution fusion | flops 7250116608 | bytes 24772608 | tf_op jit(solution)/shard_map/dot_general | solution.py:14
  251.3 0.0 copy-start
  251.3 0.0 reduce-scatter.6.cloned.1.call-update
  251.3 0.0 all-gather.8.cloned.1.call-start
  251.3 49.5 %reduce-scatter.6.cloned.1.call-done = bf16[384,1536]{1,0:T(8,128)(2,1)} async-done(((bf16[384,6144]{1,0:T(8,128)(2,1)}), bf16[384,1536]{1,0:T(8,128)(2,1)}) %reduce-scatter.6.cloned.1.call-update) | async-done | bytes 1179664 | tf_op jit(solution)/shard_map/reduce_scatter | solution.py:15
  300.8 0.0 copy-done
  300.8 4.5 fusion.4
  305.3 0.0 all-gather.8.cloned.1.call-update
  305.4 0.0 reduce-scatter.10.cloned.1.call-start
  305.4 52.4 %all-gather.8.cloned.1.call-done = bf16[384,6144]{1,0:T(8,128)(2,1)} async-done(((bf16[384,1536]{1,0:T(8,128)(2,1)}), bf16[384,6144]{1,0:T(8,128)(2,1)}) %all-gather.8.cloned.1.call-update) | async-done | bytes 4718608 | tf_op jit(solution)/shard_map/all_gather | solution.py:21
  357.8 12.8 %convolution_convert_fusion.2 = bf16[384,1536]{1,0:T(8,128)(2,1)S(1)} fusion(bf16[384,6144]{1,0:T(8,128)(2,1)} %all-gather.8.cloned.1.call-done, bf16[1536,6144]{1,0:T(8,128)(2,1)} %all-gather.6.cloned.1.call-done), kind=kOutput, calls=%fused_computation.10 | convolution fusion | flops 7248347136 | bytes 24772608 | tf_op jit(solution)/shard_map/dot_general | solution.py:22
  370.6 0.0 copy-start.1
  370.6 1.4 copy.8
  372.0 0.0 reduce-scatter.10.cloned.1.call-update
  372.1 0.2 reduce-scatter.8.cloned.1.call-start
  372.3 0.0 copy-done.1
  372.3 15.5 %fusion = bf16[1536,6144]{0,1:T(8,128)(2,1)} fusion(bf16[384,6144]{1,0:T(8,128)(2,1)} %all-gather.8.cloned.1.call-done, bf16[384,1536]{1,0:T(8,128)(2,1)S(1)} %copy-done.1), kind=kOutput, calls=%fused_computation.1 | convolution fusion | flops 7257194496 | bytes 24772608 | tf_op jit(solution)/shard_map/dot_general | solution.py:28
  387.8 0.0 reduce-scatter.8.cloned.1.call-update
  387.8 5.8 reduce-scatter.10.cloned.1.call-done
  393.7 1.8 copy.9
  395.5 210.2 %reduce-scatter.8.cloned.1.call-done = bf16[1536,768]{0,1:T(8,128)(2,1)} async-done(((bf16[1536,6144]{0,1:T(8,128)(2,1)}), bf16[1536,768]{0,1:T(8,128)(2,1)}) %reduce-scatter.8.cloned.1.call-update) | async-done | bytes 2359312 | tf_op jit(solution)/shard_map/reduce_scatter | solution.py:31
  605.7 4.3 copy.7
Async XLA Ops:
  7.2 27.7 %all-gather.4.cloned.1.call-start = ((), (), s32[]{:S(2)}) async-start(), calls=%async_computation.3 | async-start | bytes 1474560 | tf_op jit(solution)/shard_map/all_gather | solution.py:12
  7.9 230.3 %all-gather.6.cloned.1.call-start = ((), (), s32[]{:S(2)}) async-start(), calls=%async_computation.4 | async-start | bytes 21233664 | tf_op jit(solution)/shard_map/all_gather | solution.py:13
  8.6 292.1 %reduce-scatter.6.cloned.1.call-start = ((), (), s32[]{:S(2)}) async-start(), calls=%async_computation.5 | async-start | bytes 5898240 | tf_op jit(solution)/shard_map/reduce_scatter | solution.py:15
  251.3 49.5 %copy-start = (bf16[384,1536]{1,0:T(8,128)(2,1)S(1)}, bf16[384,1536]{1,0:T(8,128)(2,1)}, u32[]{:S(2)}) copy-start(bf16[384,1536]{1,0:T(8,128)(2,1)} %param.5) | copy-start | bytes 3538948
  251.3 106.5 %all-gather.8.cloned.1.call-start = ((), (), s32[]{:S(2)}) async-start(), calls=%async_computation.6 | async-start | bytes 5898240 | tf_op jit(solution)/shard_map/all_gather | solution.py:21
  305.4 88.3 %reduce-scatter.10.cloned.1.call-start = ((), (), s32[]{:S(2)}) async-start(), calls=%async_computation.8 | async-start | bytes 1474560
  370.6 1.7 copy-start.1
  372.1 233.7 %reduce-scatter.8.cloned.1.call-start = ((), (), s32[]{:S(2)}) async-start(), calls=%async_computation.7 | async-start | bytes 21233664 | tf_op jit(solution)/shard_map/reduce_scatter | solution.py:31
Sparse Core Ops, SparseCore 0:
  9.7 25.1 all-gather.3
  37.2 200.9 all-gather.5
  251.4 49.3 reduce-scatter.5
  305.5 52.2 all-gather.7
  372.2 21.4 reduce-scatter.9
  397.5 208.1 reduce-scatter.7
where the time goes:
time: 618 us; the launch traced here: 617 us
  waiting for transfers between devices  549 us (89%)
  matrix products  41.4 us (7%)
  between operations  14.1 us (2%)
  local copies, waits for them, and re-layouts  7.53 us (1%)
    reduce_scatter x1, waiting for transfers between devices, on_device(): lax.psum_scatter(weight_terms.astype(jnp.bfloat16), 'gy', scatter_dimensi...  210 us
    all_gather x1, waiting for transfers between devices, on_device(): weight_cols = lax.all_gather(weight, 'gy', axis=1, tiled=True)  203 us
    all_gather x1, waiting for transfers between devices, on_device(): slopes = lax.all_gather(own_slopes, 'gz', axis=1, tiled=True)  52.4 us
    reduce_scatter x1, waiting for transfers between devices, on_device(): lax.psum_scatter(partial_value.astype(jnp.bfloat16), 'gz', scatter_dimens...  49.5 us
    all_gather x1, waiting for transfers between devices, on_device(): row_inputs = lax.all_gather(inputs, 'gx', axis=1, tiled=True)  26.2 us
    dot_general x1, matrix products, on_device(): lax.dot_general(row_inputs, slopes, (((0,), (0,)), ((), ())), preferred_e...  15.5 us
    dot_general x1, matrix products, on_device(): jnp.dot(row_inputs, weight_cols, preferred_element_type=jnp.float32)  13 us
    dot_general x1, matrix products, on_device(): lax.dot_general(slopes, weight_cols, (((1,), (1,)), ((), ())), preferred_...  12.8 us
  transfers between devices with their start and end apart: 6, of which 6 were waited for; matrix products, arithmetic and copies ran while one was open for 3% of the time, Pallas kernels for 0%

commit v1 on v0

v1 whole, which is shorter than its diff:
```python
import functools

import jax
import jax.numpy as jnp
from jax import lax
from jax.experimental import pallas as pl
from jax.experimental.pallas import tpu as pltpu
from jax.sharding import PartitionSpec as P

MESH = pl.DeviceIdType.MESH
F32, BF16 = jnp.float32, jnp.bfloat16
RING = 4
SPANS = (16, 32, 32, 16)
OWN = sum(SPANS)
STARTS = tuple(sum(SPANS[:k]) for k in range(len(SPANS)))
CHUNKS = range(len(SPANS))
HID = 768
FEAT = 384
N_SEM = 320
N_LOCAL = 40


def part_of(first, step):
    return pl.ds(first, step)


class Device:
    def __init__(self):
        gx, gy, gz = (lax.axis_index(name) for name in ("gx", "gy", "gz"))
        self.core = gx % 2
        self.at = {"x": (gy % 2) * 2 + gx // 2, "y": gz, "z": gy // 2}

    def name(self, core=None, **at):
        at = {**self.at, **at}
        core = self.core if core is None else core
        return {"gx": (at["x"] % 2) * 2 + core, "gy": at["z"] * 2 + at["x"] // 2, "gz": at["y"]}

    def along(self, axis, step):
        return (self.at[axis] + step) % RING


def cols(x):
    return pl.ds(pl.multiple_of((x % 2) * FEAT, FEAT), FEAT)


def gelu_and_slope(value, cotangent):
    scale, cubic = 0.7978845608028654, 0.044715
    square = value * value
    t = jnp.tanh(scale * value * (1.0 + cubic * square))
    half = 0.5 * (1.0 + t)
    slope = half + 0.5 * value * ((1.0 + t) * (1.0 - t)) * (scale + (3.0 * cubic * scale) * square)
    return value * half, cotangent * slope


def add_into(dst, *srcs):
    total = dst[...].astype(F32)
    for src in srcs:
        total = total + src[...].astype(F32)
    dst[...] = total.astype(BF16)


def add_rows(dst, *srcs):
    def step(i, carry):
        add_into(dst.at[i], *(src.at[i] for src in srcs))
        return carry

    lax.fori_loop(0, dst.shape[0], step, 0)


class Moves:
    def __init__(self, device, send, recv, local):
        self.device, self.send, self.recv, self.local = device, send, recv, local
        self.count = self.locals = 0
        self.sent = []

    def start(self, src, dst, **to):
        j = self.count
        self.count += 1
        copy = pltpu.make_async_remote_copy(
            src_ref=src, dst_ref=dst, send_sem=self.send.at[j], recv_sem=self.recv.at[j],
            device_id=self.device.name(**to), device_id_type=MESH,
        )
        copy.start()
        self.sent.append(copy)
        return copy

    def here(self, src, dst):
        j = self.locals
        self.locals += 1
        copy = pltpu.make_async_copy(src, dst, self.local.at[j])
        copy.start()
        return copy

    def drain(self):
        for copy in self.sent:
            copy.wait_send()
        self.sent = []


class Gather:
    def __init__(self, moves, axis, slot, own=None):
        self.m, self.axis, self.slot = moves, axis, slot
        self.own = own or (lambda part: slot(moves.device.at[axis], part))

    def begin(self):
        d, a = self.m.device, self.axis
        me = d.at[a]
        up, down = {a: d.along(a, 1)}, {a: d.along(a, 3)}
        self.up0 = self.m.start(self.own(0), self.slot(me, 0), **up)
        self.down1 = self.m.start(self.own(1), self.slot(me, 1), **down)
        self.up1 = self.m.start(self.own(1), self.slot(me, 1), **up)
        self.down0 = self.m.start(self.own(0), self.slot(me, 0), **down)

    def forward(self):
        d, a = self.m.device, self.axis
        self.up0.wait_recv()
        view = self.slot(d.along(a, 3), 0)
        self.far0 = self.m.start(view, view, **{a: d.along(a, 1)})
        self.down1.wait_recv()
        view = self.slot(d.along(a, 1), 1)
        self.far1 = self.m.start(view, view, **{a: d.along(a, 3)})

    def end(self):
        for copy in (self.up1, self.down0, self.far0, self.far1):
            copy.wait_recv()


class Reduce:
    def __init__(self, moves, axis, piece, far, near, add):
        self.m, self.axis, self.piece, self.far, self.near, self.add = moves, axis, piece, far, near, add

    def begin(self):
        d, a, p = self.m.device, self.axis, self.piece
        up, down, across = d.along(a, 1), d.along(a, 3), d.along(a, 2)
        self.far0 = self.m.start(p(across, 0), self.far.at[0], **{a: up})
        self.far1 = self.m.start(p(across, 1), self.far.at[1], **{a: down})
        self.up1 = self.m.start(p(up, 1), self.near.at[0, 1], **{a: up})
        self.down0 = self.m.start(p(down, 0), self.near.at[1, 0], **{a: down})

    def middle(self):
        d, a, p = self.m.device, self.axis, self.piece
        up, down = d.along(a, 1), d.along(a, 3)
        self.far0.wait_recv()
        self.add(p(up, 0), self.far.at[0])
        self.up0 = self.m.start(p(up, 0), self.near.at[0, 0], **{a: up})
        self.far1.wait_recv()
        self.add(p(down, 1), self.far.at[1])
        self.down1 = self.m.start(p(down, 1), self.near.at[1, 1], **{a: down})

    def arrive(self):
        for copy in (self.up0, self.up1, self.down0, self.down1):
            copy.wait_recv()

    def end(self):
        self.arrive()
        me = self.m.device.at[self.axis]
        for part in range(2):
            self.add(self.piece(me, part), self.near.at[0, part], self.near.at[1, part])


def scratch_of():
    shapes = {}
    for k in CHUNKS:
        r = SPANS[k]
        block = (4, 2, 4, r, HID)
        for name, shape in dict(
            x=(2, *block), p=block, s=block, d=(2, *block), core=block,
            yfar=(2, 2, 2, r, HID), ynear=(2, 2, 2, 2, r, HID),
            axfar=(2, 2, 2, r, FEAT), axnear=(2, 2, 2, 2, r, FEAT),
            azfar=(2, 1, r, FEAT), aznear=(2, 2, 1, r, FEAT),
            bzfar=(2, 1, 2, r, HID), bznear=(2, 2, 1, 2, r, HID),
            bxfar=(2, 1, r, FEAT), bxnear=(2, 2, 1, r, FEAT),
        ).items():
            shapes.setdefault(name, []).append(shape)
    return shapes


NAMES = tuple(scratch_of())


def kernel(in_ref, w_ref, cot_ref, act_ref, dx_ref, dw_ref, *scratch):
    bufs, rest = {}, list(scratch)
    for name in NAMES:
        bufs[name] = [rest.pop(0) for _ in CHUNKS]
    w, acc, dw, cot1, cot, act, act1, send, recv, local = rest
    dev = Device()
    core, at = dev.core, dev.at
    x, y, z = at["x"], at["y"], at["z"]
    half = x // 2
    m = Moves(dev, send, recv, local)
    plane = [(dz, dh) for dz in range(4) for dh in range(2) if (dz, dh) != (0, 0)]

    def in_plane(dz, dh):
        return dict(z=(z + dz) % RING, x=((half + dh) % 2) * 2 + x % 2)

    w_copies = [m.here(w_ref.at[lo, c], w.at[c, pl.ds(lo * FEAT, FEAT)]) for c in range(2) for lo in range(2)]
    own_copies = [
        m.here(in_ref.at[:, pl.ds(STARTS[k], SPANS[k])], bufs["x"][k].at[core, z, half, :, :, cols(x)]) for k in CHUNKS
    ]

    barrier = pltpu.get_barrier_semaphore()
    peers = [dict(core=1 - core), dict(x=dev.along("x", 1)), dict(x=dev.along("x", 3))]
    peers += [dict(y=dev.along("y", s)) for s in (1, 2, 3)] + [in_plane(*step) for step in plane]
    for peer in peers:
        pl.semaphore_signal(barrier, inc=1, device_id=dev.name(**peer), device_id_type=MESH)
    pl.semaphore_wait(barrier, len(peers))

    gathers = {}

    def input_gathers(k):
        b = bufs["x"][k]
        rows = pl.ds(STARTS[k], SPANS[k])

        def own(first):
            return lambda part: in_ref.at[pl.ds(first + part, 1), rows]

        gathers[k] = dict(
            ax=Gather(m, "x", lambda q, part: b.at[core, z, q // 2, pl.ds(part, 1), :, cols(q)], own(0)),
            az=Gather(m, "z", lambda q, part: b.at[core, q, part, pl.ds(0, 2)]),
            bz=Gather(m, "z", lambda q, part: b.at[core, q, half, pl.ds(2 + part, 1), :, cols(x)], own(2)),
            bx=Gather(m, "x", lambda q, part: b.at[core, pl.ds(2 * part, 2), q // 2, pl.ds(2, 2), :, cols(q)]),
        )

    def xa(k, stage):
        b = bufs["x"][k]
        if stage == 0:
            input_gathers(k)
            g = gathers[k]
            g["ax"].begin()
            g["bz"].begin()
        g = gathers[k]
        if stage == 1:
            g["ax"].forward()
            g["bz"].forward()
        if stage == 2:
            own_copies[k].wait()
            g["ax"].end()
            g["az"].begin()
            g["bz"].end()
            g["bx"].begin()
        if stage == 3:
            g["az"].forward()
            g["bx"].forward()
        if stage == 4:
            g["az"].end()
            view = b.at[core, :, :, pl.ds(0, 2)]
            g["core0"] = m.start(view, view, core=1 - core)
            g["bx"].end()
            view = b.at[core, :, :, pl.ds(2, 2)]
            g["core1"] = m.start(view, view, core=1 - core)
        if stage == 5:
            g["core0"].wait_recv()
            g["core1"].wait_recv()

    cot_moves = {}

    def cot_y():
        cot_moves["own"] = m.here(cot_ref.at[y], cot1.at[y])
        cot_moves["y"] = [
            m.start(cot_ref.at[dev.along("y", s)], cot1.at[y], y=dev.along("y", s)) for s in (1, 2, 3)
        ]

    def cot_plane():
        cot_moves["own"].wait()
        for copy in cot_moves["y"]:
            copy.wait_recv()

        def source(to):
            return cot1.at[to["z"], :, pl.ds(pl.multiple_of((to["x"] // 2) * HID, HID), HID)]

        cot_moves["plane"] = [m.start(source(in_plane(*step)), cot.at[z, half], **in_plane(*step)) for step in plane]
        cot_moves["plane_own"] = m.here(source(dict(z=z, x=x)), cot.at[z, half])

    def cot_end():
        cot_moves["plane_own"].wait()
        for copy in cot_moves["plane"]:
            copy.wait_recv()

    act_moves = {}

    def act_plane(first, count):
        rows = pl.ds(first, count)
        dst = act1.at[z, rows, pl.ds(pl.multiple_of(half * HID, HID), HID)]
        act_moves[first] = [
            m.start(act.at[to["z"], to["x"] // 2, rows], dst, **to) for to in (in_plane(*step) for step in plane)
        ], m.here(act.at[z, half, rows], dst)

    def act_y(first, count):
        rows = pl.ds(first, count)
        remote, mine = act_moves[first]
        mine.wait()
        for copy in remote:
            copy.wait_recv()
        act_moves[first] = [
            m.start(act1.at[dev.along("y", s), rows], act_ref.at[y, rows], y=dev.along("y", s)) for s in (1, 2, 3)
        ], m.here(act1.at[y, rows], act_ref.at[y, rows])

    def act_end(first):
        remote, mine = act_moves[first]
        mine.wait()
        for copy in remote:
            copy.wait_recv()

    sums = {}

    def project(k):
        b, p, r = bufs["x"][k], bufs["p"][k], SPANS[k]
        if k == 0:
            for copy in w_copies:
                copy.wait()

        def tile(n, carry):
            where = pl.ds(pl.multiple_of(n * 256, 256), 256)
            total = jnp.dot(b[0].reshape(32 * r, HID), w[0, :, where], preferred_element_type=F32)
            total += jnp.dot(b[1].reshape(32 * r, HID), w[1, :, where], preferred_element_type=F32)
            p[:, :, :, :, where] = total.astype(BF16).reshape(4, 2, 4, r, 256)
            return carry

        lax.fori_loop(0, 3, tile, 0)
        sums[k] = Reduce(
            m, "y", lambda q, part: p.at[pl.ds(2 * part, 2), :, q], bufs["yfar"][k], bufs["ynear"][k], add_rows
        )
        sums[k].begin()

    spread = {}

    def gelu(k):
        p, s, near, r = bufs["p"][k], bufs["s"][k], bufs["ynear"][k], SPANS[k]
        sums[k].arrive()
        rows = pl.ds(STARTS[k], r)

        def step(i, carry):
            zz, hh = i // 2, i % 2
            value = p[zz, hh, y].astype(F32)
            value = value + near[0, zz // 2, zz % 2, hh].astype(F32) + near[1, zz // 2, zz % 2, hh].astype(F32)
            a, slope = gelu_and_slope(value, cot[zz, hh, rows].astype(F32))
            act[zz, hh, rows] = a.astype(BF16)
            s[zz, hh, y] = slope.astype(BF16)
            return carry

        lax.fori_loop(0, 8, step, 0)
        spread[k] = Gather(m, "y", lambda q, part: s.at[pl.ds(2 * part, 2), :, q])
        spread[k].begin()

    crossing = {}

    def input_terms(k):
        s, d, r = bufs["s"][k], bufs["d"][k], SPANS[k]
        spread[k].end()

        def one(c):
            def tile(n, carry):
                where = pl.ds(pl.multiple_of(n * 256, 256), 256)
                total = lax.dot_general(
                    s[...].reshape(32 * r, HID), w[c, where, :], (((1,), (1,)), ((), ())), preferred_element_type=F32
                )
                d[c, :, :, :, :, where] = total.astype(BF16).reshape(4, 2, 4, r, 256)
                return carry

            lax.fori_loop(0, 3, tile, 0)

        one(1 - core)
        crossing[k] = m.start(d.at[1 - core], bufs["core"][k], core=1 - core)
        one(core)

    def weight_terms(k):
        b, s, r = bufs["x"][k], bufs["s"][k], SPANS[k]

        def tile(n, carry):
            c = n // 3
            where = pl.ds(pl.multiple_of((n % 3) * 256, 256), 256)
            total = lax.dot_general(
                b[c, :, :, :, :, where].reshape(32 * r, 256), s[...].reshape(32 * r, HID),
                (((0,), (0,)), ((), ())), preferred_element_type=F32,
            )
            if k > 0:
                total = total + acc[c, where, :]
            if k < len(SPANS) - 1:
                acc[c, where, :] = total
            else:
                dw[c, where, :] = total.astype(BF16)
            return carry

        lax.fori_loop(0, 6, tile, 0)

    def weight_out():
        return [m.here(dw.at[c, pl.ds(lo * FEAT, FEAT)], dw_ref.at[lo, c]) for c in range(2) for lo in range(2)]

    backs = {}

    def dxs(k, stage):
        d, r = bufs["d"][k], SPANS[k]
        if stage == 0:
            crossing[k].wait_recv()
            add_rows(d.at[core], bufs["core"][k])
            backs[k] = dict(
                ax=Reduce(m, "x", lambda q, part: d.at[core, pl.ds(2 * part, 2), q // 2, pl.ds(0, 2), :, cols(q)],
                          bufs["axfar"][k], bufs["axnear"][k], add_into),
                bz=Reduce(m, "z", lambda q, part: d.at[core, q, pl.ds(part, 1), pl.ds(2, 2)],
                          bufs["bzfar"][k], bufs["bznear"][k], add_into),
                az=Reduce(m, "z", lambda q, part: d.at[core, q, half, pl.ds(part, 1), :, cols(x)],
                          bufs["azfar"][k], bufs["aznear"][k], add_into),
                bx=Reduce(m, "x", lambda q, part: d.at[core, z, q // 2, pl.ds(2 + part, 1), :, cols(q)],
                          bufs["bxfar"][k], bufs["bxnear"][k], add_into),
            )
            backs[k]["ax"].begin()
            backs[k]["bz"].begin()
        g = backs[k]
        if stage == 1:
            g["ax"].middle()
            g["bz"].middle()
        if stage == 2:
            g["ax"].end()
            g["az"].begin()
            g["bz"].end()
            g["bx"].begin()
        if stage == 3:
            g["az"].middle()
            g["bx"].middle()
        if stage == 4:
            g["az"].end()
            g["bx"].end()
            dx_ref[:, pl.ds(STARTS[k], r), :] = d[core, z, half, :, :, cols(x)]

    last = len(SPANS) - 1
    xa(0, 0)
    cot_y()
    xa(0, 1)
    xa(0, 2)
    xa(1, 0)
    xa(0, 3)
    xa(1, 1)
    xa(0, 4)
    xa(1, 2)
    xa(0, 5)
    project(0)
    xa(1, 3)
    cot_plane()
    xa(1, 4)
    sums[0].middle()
    xa(2, 0)
    xa(1, 5)
    project(1)
    xa(2, 1)
    cot_end()
    for k in CHUNKS:
        gelu(k)
        if k + 1 <= last:
            sums[k + 1].middle()
        if k + 2 <= last:
            xa(k + 2, 2)
            xa(k + 2, 3)
            if k + 3 <= last:
                xa(k + 3, 0)
        spread[k].forward()
        if k + 2 <= last:
            xa(k + 2, 4)
            xa(k + 2, 5)
            project(k + 2)
            if k + 3 <= last:
                xa(k + 3, 1)
        if k == last - 1:
            act_plane(0, STARTS[last])
        if k >= 1:
            dxs(k - 1, 1)
            dxs(k - 1, 2)
        if k == last:
            act_plane(STARTS[last], SPANS[last])
        input_terms(k)
        dxs(k, 0)
        if k >= 1:
            dxs(k - 1, 3)
        weight_terms(k)
        if k >= 1:
            dxs(k - 1, 4)
    act_y(0, STARTS[last])
    act_y(STARTS[last], SPANS[last])
    outs = weight_out()
    for stage in (1, 2, 3, 4):
        dxs(last, stage)
    act_end(0)
    act_end(STARTS[last])
    for copy in outs:
        copy.wait()
    m.drain()


def on_device(inputs, weight, cotangent):
    shapes = [pltpu.VMEM(shape, BF16) for name, each in scratch_of().items() for shape in each]
    act, dx, dw = pl.pallas_call(
        kernel,
        out_shape=(
            jax.ShapeDtypeStruct((4, OWN, 2 * HID), BF16),
            jax.ShapeDtypeStruct((4, OWN, FEAT), BF16),
            jax.ShapeDtypeStruct((2, 2, FEAT, HID), BF16),
        ),
        in_specs=[
            pl.BlockSpec(memory_space=pltpu.VMEM),
            pl.BlockSpec(memory_space=pl.ANY),
            pl.BlockSpec(memory_space=pl.ANY),
        ],
        out_specs=(
            pl.BlockSpec(memory_space=pl.ANY),
            pl.BlockSpec(memory_space=pltpu.VMEM),
            pl.BlockSpec(memory_space=pl.ANY),
        ),
        scratch_shapes=[
            *shapes,
            pltpu.VMEM((2, HID, HID), BF16),
            pltpu.VMEM((2, HID, HID), F32),
            pltpu.VMEM((2, HID, HID), BF16),
            pltpu.VMEM((4, OWN, 2 * HID), BF16),
            pltpu.VMEM((4, 2, OWN, HID), BF16),
            pltpu.VMEM((4, 2, OWN, HID), BF16),
            pltpu.VMEM((4, OWN, 2 * HID), BF16),
            pltpu.SemaphoreType.DMA((N_SEM,)),
            pltpu.SemaphoreType.DMA((N_SEM,)),
            pltpu.SemaphoreType.DMA((N_LOCAL,)),
        ],
        compiler_params=pltpu.CompilerParams(
            collective_id=0, has_side_effects=True, vmem_limit_bytes=62 * 2**20
        ),
        cost_estimate=pl.CostEstimate(flops=6 * 384 * 1536 * 6144, bytes_accessed=8 * 2**20, transcendentals=0),
    )(
        inputs.reshape(4, OWN, FEAT),
        weight.reshape(2, 2, FEAT, HID),
        cotangent.reshape(4, OWN, 2 * HID),
    )
    return act.reshape(4 * OWN, 2 * HID), dx.reshape(4 * OWN, FEAT), dw.reshape(4 * FEAT, HID)


def solution(mesh):
    return jax.shard_map(
        on_device,
        mesh=mesh,
        in_specs=(P("gy", ("gz", "gx")), P("gz", ("gx", "gy")), P("gy", ("gx", "gz"))),
        out_specs=(P("gy", ("gx", "gz")), P("gy", ("gz", "gx")), P("gz", ("gx", "gy"))),
        check_vma=False,
    )
```

time: 618 us -> 194 us (0.31)
  waiting for transfers between devices: 549 us -> 0 us
  Pallas kernels: 0 us -> 187 us
  matrix products: 41.4 us -> 0 us
  between operations: 14.1 us -> 0.65 us
    all_gather x3 -> x0, waiting for transfers between devices: 282 us -> none  [the longest x1 203 us: on_device(): weight_cols = lax.all_gather(weight, 'gy', axis=1, tiled=True)]
    reduce_scatter x2 -> x0, waiting for transfers between devices: 260 us -> none  [the longest x1 210 us: on_device(): lax.psum_scatter(weight_terms.astype(jnp.bfloat16), 'gy', scatter_dimensi...]
    pallas_call x0 -> x1, Pallas kernels: none -> 187 us  [on_device(): pl.pallas_call(kernel, out_shape=(jax.ShapeDtypeStruct((4, OWN, 2 * HID),...]
    dot_general x3 -> x0, matrix products: 41.4 us -> none  [the longest x1 15.5 us: on_device(): lax.dot_general(row_inputs, slopes, (((0,), (0,)), ((), ())), preferred_e...]
    unnamed x7 -> x0, waiting for transfers between devices: 7.28 us -> none
  transfers between devices with their start and end apart: 6 -> 0, of which waited for: 6 -> 0; matrix products, arithmetic and copies ran while one was open for 3% -> 0% of each run, Pallas kernels for 0% -> 0%
where the time goes in v1:
time: 194 us; the launch traced here: 193 us
  Pallas kernels  187 us (96%)
  local copies, waits for them, and re-layouts  5.62 us (3%)
    pallas_call x1, Pallas kernels, on_device(): pl.pallas_call(kernel, out_shape=(jax.ShapeDtypeStruct((4, OWN, 2 * HID),...  187 us
    unnamed x5, local copies, waits for them, and re-layouts  5.62 us

profile of v1, /device:TPU:1, one launch (start us, length us, event | category | flops | bytes accessed | tf_op | source)
XLA Modules:
  0.0 193.5 jit_solution(11912558226021378688)
XLA Ops:
  0.6 187.2 %shard_map.58 = (bf16[4,96,1536]{2,1,0:T(8,128)(2,1)}, bf16[4,96,384]{2,1,0:T(8,128)(2,1)}, bf16[2,2,384,768]{3,2,1,0:T(8,128)(2,1)}) custom-call(bf16[4,96,384]{2,1,0:T(8,128)(2,1)} %bitcast.11, bf16[2,2,384,768]{3,2,1,0:T(8,128)(2,1)} %bitcast.9, bf16[4,96,1536]{2,1,0:T(8,128)(2,1)} %bitcast.10), custom_call_target="tpu_custom_call" | custom-call | flops 21743271936 | bytes 8388608 | tf_op jit(solution)/shard_map/pallas_call | solution.py:490
  187.8 0.0 copy-start
  187.8 2.5 %copy.9 = bf16[384,1536]{1,0:T(8,128)(2,1)} copy(bf16[384,1536]{1,0:T(8,128)(2,1)} %bitcast.7) | data formatting | bytes 2359296
  190.4 1.7 copy.10
  192.1 0.0 copy-done
  192.1 1.4 copy.11
Async XLA Ops:
  187.8 4.2 %copy-start = (bf16[2,2,384,768]{3,2,1,0:T(8,128)(2,1)S(1)}, bf16[2,2,384,768]{3,2,1,0:T(8,128)(2,1)}, u32[]{:S(2)}) copy-start(bf16[2,2,384,768]{3,2,1,0:T(8,128)(2,1)} %get-tuple-element.8) | copy-start | bytes 7077892

commit v2 on v0

v2 whole, which is shorter than its diff:
```python
import functools

import jax
import jax.numpy as jnp
from jax import lax
from jax.experimental import pallas as pl
from jax.experimental.pallas import tpu as pltpu
from jax.sharding import PartitionSpec as P

MESH = pl.DeviceIdType.MESH
F32, BF16 = jnp.float32, jnp.bfloat16
RING = 4
SPANS = (16, 16, 16, 16, 16, 16)
OWN = sum(SPANS)
STARTS = tuple(sum(SPANS[:k]) for k in range(len(SPANS)))
CHUNKS = range(len(SPANS))
HID = 768
FEAT = 384
N_SEM = 512
N_LOCAL = 64
COT_PARTS = ((0, 1), (1, 6))
ACT_PARTS = ((0, 5), (5, 6))
DIRECT_IN = (0, 1, 2, 3, 4, 5)
DIRECT_OUT = (0, 1, 2, 3, 4, 5)
ORDER = (
    ("ax0", 0), ("bz0", 0), ("bz0", 1), ("bz0", 2), ("ax0", 1), ("ax0", 2), ("c0", 0), ("c0", 1), ("ax0", 3),
    ("bz0", 3), ("ax2", 0), ("bz2", 0), ("ax2", 1), ("bz2", 1), ("bz0", 4), ("bz2", 2), ("ax2", 2),
    ("bz0", 5), ("c1", 0), ("az2", 0), ("bx2", 0), ("ax0", 4), ("P", 0), ("az2", 1), ("bz2", 3), ("ax2", 3),
    ("bx2", 1), ("P", 1), ("c1", 1), ("R1a", 0), ("bx2", 2), ("az2", 2), ("R1b", 0), ("P", 2), ("G", 0),
    ("ax0", 5), ("bz2", 5), ("R1b", 2), ("bx2", 3), ("R1a", 1), ("R1a", 2), ("az2", 3), ("ax2", 4),
    ("A1a", 0), ("R1b", 1), ("bz2", 4), ("P", 3), ("A1b", 0), ("G", 2), ("ax2", 5), ("G", 1), ("Dh", 0),
    ("Dl", 0), ("A1a", 2), ("az2", 4), ("az2", 5), ("bx2", 4), ("R1a", 3), ("bx2", 5), ("A1b", 2), ("dx0", 0),
    ("P", 4), ("P", 5), ("Dh", 2), ("Dl", 2), ("rz2", 0), ("dx0", 2), ("R1b", 3), ("rx2", 0), ("R1a", 4),
    ("R1b", 4), ("R1b", 5), ("A1a", 1), ("W", 0), ("A1b", 1), ("R1a", 5), ("G", 4), ("rz2", 2), ("G", 3),
    ("p0", 0), ("Dh", 1), ("Dl", 1), ("rx2", 2), ("A1b", 4), ("A1a", 4), ("dx0", 1), ("W", 1), ("A1a", 3),
    ("A1b", 3), ("G", 5), ("W", 2), ("p0", 1), ("sz2", 0), ("Dh", 4), ("Dl", 4), ("Dh", 3), ("dx0", 4),
    ("A1b", 5), ("A1a", 5), ("p1", 0), ("W", 3), ("Dl", 3), ("dx0", 3), ("Dh", 5), ("sz2", 2), ("Dl", 5),
    ("rz2", 4), ("p1", 1), ("dx0", 5), ("rx2", 4), ("W", 4), ("sx2", 0), ("rz2", 1), ("rx2", 3), ("rz2", 3),
    ("W", 5), ("rx2", 1), ("sx2", 2), ("rz2", 5), ("rx2", 5), ("sz2", 4), ("sx2", 4), ("sz2", 1), ("sx2", 3),
    ("sx2", 1), ("p2", 0), ("sz2", 3), ("p2", 1), ("sx2", 5), ("sz2", 5),
)


class Device:
    def __init__(self):
        gx, gy, gz = (lax.axis_index(name) for name in ("gx", "gy", "gz"))
        self.core = gx % 2
        self.at = {"x": (gy % 2) * 2 + gx // 2, "y": gz, "z": gy // 2}

    def name(self, core=None, **at):
        at = {**self.at, **at}
        core = self.core if core is None else core
        return {"gx": (at["x"] % 2) * 2 + core, "gy": at["z"] * 2 + at["x"] // 2, "gz": at["y"]}

    def along(self, axis, step):
        return (self.at[axis] + step) % RING


def cols(x):
    return pl.ds(pl.multiple_of((x % 2) * FEAT, FEAT), FEAT)


def gelu_and_slope(value, cotangent):
    scale, cubic = 0.7978845608028654, 0.044715
    square = value * value
    t = jnp.tanh(scale * value * (1.0 + cubic * square))
    half = 0.5 * (1.0 + t)
    slope = half + 0.5 * value * ((1.0 + t) * (1.0 - t)) * (scale + (3.0 * cubic * scale) * square)
    return value * half, cotangent * slope


def add_into(dst, *srcs):
    total = dst[...].astype(F32)
    for src in srcs:
        total = total + src[...].astype(F32)
    dst[...] = total.astype(BF16)


def add_rows(dst, *srcs):
    def step(i, carry):
        add_into(dst.at[i], *(src.at[i] for src in srcs))
        return carry

    lax.fori_loop(0, dst.shape[0], step, 0)


class Moves:
    def __init__(self, device, send, recv, local):
        self.device, self.send, self.recv, self.local = device, send, recv, local
        self.count = self.locals = 0
        self.sent = []

    def start(self, src, dst, **to):
        j = self.count
        self.count += 1
        copy = pltpu.make_async_remote_copy(
            src_ref=src, dst_ref=dst, send_sem=self.send.at[j], recv_sem=self.recv.at[j],
            device_id=self.device.name(**to), device_id_type=MESH,
        )
        copy.start()
        self.sent.append(copy)
        return copy

    def here(self, src, dst):
        j = self.locals
        self.locals += 1
        copy = pltpu.make_async_copy(src, dst, self.local.at[j])
        copy.start()
        return copy

    def drain(self):
        for copy in self.sent:
            copy.wait_send()
        self.sent = []


class Gather:
    def __init__(self, moves, axis, slot, own=None, direct=False):
        self.m, self.axis, self.slot, self.direct = moves, axis, slot, direct
        self.own = own or (lambda part: slot(moves.device.at[axis], part))

    def begin(self):
        d, a = self.m.device, self.axis
        me = d.at[a]
        if self.direct:
            self.copies = [
                self.m.start(self.own(part), self.slot(me, part), **{a: d.along(a, step)})
                for part in range(2) for step in (1, 3, 2)
            ]
            return
        up, down = {a: d.along(a, 1)}, {a: d.along(a, 3)}
        self.up0 = self.m.start(self.own(0), self.slot(me, 0), **up)
        self.down1 = self.m.start(self.own(1), self.slot(me, 1), **down)
        self.up1 = self.m.start(self.own(1), self.slot(me, 1), **up)
        self.down0 = self.m.start(self.own(0), self.slot(me, 0), **down)

    def forward_up(self):
        d, a = self.m.device, self.axis
        self.up0.wait_recv()
        view = self.slot(d.along(a, 3), 0)
        self.far0 = self.m.start(view, view, **{a: d.along(a, 1)})

    def forward_down(self):
        d, a = self.m.device, self.axis
        self.down1.wait_recv()
        view = self.slot(d.along(a, 1), 1)
        self.far1 = self.m.start(view, view, **{a: d.along(a, 3)})

    def end(self):
        for copy in self.copies if self.direct else (self.up1, self.down0, self.far0, self.far1):
            copy.wait_recv()


class Reduce:
    def __init__(self, moves, axis, piece, far, near, add, direct=False):
        self.m, self.axis, self.piece, self.far, self.near, self.add = moves, axis, piece, far, near, add
        self.direct = direct

    def begin(self):
        d, a, p = self.m.device, self.axis, self.piece
        up, down, across = d.along(a, 1), d.along(a, 3), d.along(a, 2)
        if self.direct:
            self.copies = [
                self.m.start(p(to, part), land, **{a: to})
                for part in range(2)
                for to, land in ((up, self.near.at[0, part]), (down, self.near.at[1, part]), (across, self.far.at[part]))
            ]
            return
        self.far0 = self.m.start(p(across, 0), self.far.at[0], **{a: up})
        self.far1 = self.m.start(p(across, 1), self.far.at[1], **{a: down})
        self.up1 = self.m.start(p(up, 1), self.near.at[0, 1], **{a: up})
        self.down0 = self.m.start(p(down, 0), self.near.at[1, 0], **{a: down})

    def middle_up(self):
        d, a, p = self.m.device, self.axis, self.piece
        up = d.along(a, 1)
        self.far0.wait_recv()
        self.add(p(up, 0), self.far.at[0])
        self.up0 = self.m.start(p(up, 0), self.near.at[0, 0], **{a: up})

    def middle_down(self):
        d, a, p = self.m.device, self.axis, self.piece
        down = d.along(a, 3)
        self.far1.wait_recv()
        self.add(p(down, 1), self.far.at[1])
        self.down1 = self.m.start(p(down, 1), self.near.at[1, 1], **{a: down})

    def arrive(self):
        for copy in self.copies if self.direct else (self.up0, self.up1, self.down0, self.down1):
            copy.wait_recv()

    def end(self):
        self.arrive()
        me = self.m.device.at[self.axis]
        for part in range(2):
            more = (self.far.at[part],) if self.direct else ()
            self.add(self.piece(me, part), self.near.at[0, part], self.near.at[1, part], *more)


def scratch_of():
    shapes = {}
    for k in CHUNKS:
        r = SPANS[k]
        block = (4, 2, 4, r, HID)
        for name, shape in dict(
            x=(2, *block), p=block, s=block, d=(2, *block), core=block,
            yfar=(2, 2, 2, r, HID), ynear=(2, 2, 2, 2, r, HID),
            axfar=(2, 2, 2, r, FEAT), axnear=(2, 2, 2, 2, r, FEAT),
            azfar=(2, 1, r, FEAT), aznear=(2, 2, 1, r, FEAT),
            bzfar=(2, 1, 2, r, HID), bznear=(2, 2, 1, 2, r, HID),
            bxfar=(2, 1, r, FEAT), bxnear=(2, 2, 1, r, FEAT),
        ).items():
            shapes.setdefault(name, []).append(shape)
    return shapes


NAMES = tuple(scratch_of())


def kernel(in_ref, w_ref, cot_ref, act_ref, dx_ref, dw_ref, *scratch):
    bufs, rest = {}, list(scratch)
    for name in NAMES:
        bufs[name] = [rest.pop(0) for _ in CHUNKS]
    w, acc, dw, cot1, cot, act, act1, send, recv, local = rest
    dev = Device()
    core, at = dev.core, dev.at
    x, y, z = at["x"], at["y"], at["z"]
    half = x // 2
    m = Moves(dev, send, recv, local)
    plane = [(dz, dh) for dz in range(4) for dh in range(2) if (dz, dh) != (0, 0)]

    def in_plane(dz, dh):
        return dict(z=(z + dz) % RING, x=((half + dh) % 2) * 2 + x % 2)

    w_copies = [m.here(w_ref.at[lo, c], w.at[c, pl.ds(lo * FEAT, FEAT)]) for c in range(2) for lo in range(2)]
    own_copies = [
        m.here(in_ref.at[:, pl.ds(STARTS[k], SPANS[k])], bufs["x"][k].at[core, z, half, :, :, cols(x)]) for k in CHUNKS
    ]

    barrier = pltpu.get_barrier_semaphore()
    peers = [dict(core=1 - core), dict(x=dev.along("x", 1)), dict(x=dev.along("x", 3))]
    peers += [dict(y=dev.along("y", s)) for s in (1, 2, 3)] + [in_plane(*step) for step in plane]
    for peer in peers:
        pl.semaphore_signal(barrier, inc=1, device_id=dev.name(**peer), device_id_type=MESH)
    pl.semaphore_wait(barrier, len(peers))

    tasks = {}

    def task(name):
        def keep(step):
            tasks[name] = step
            return step

        return keep

    def input_tasks(k):
        b = bufs["x"][k]
        rows = pl.ds(STARTS[k], SPANS[k])

        def own(first):
            return lambda part: in_ref.at[pl.ds(first + part, 1), rows]

        ax = Gather(m, "x", lambda q, part: b.at[core, z, q // 2, pl.ds(part, 1), :, cols(q)], own(0), k in DIRECT_IN)
        az = Gather(m, "z", lambda q, part: b.at[core, q, part, pl.ds(0, 2)], direct=k in DIRECT_IN)
        bz = Gather(m, "z", lambda q, part: b.at[core, q, half, pl.ds(2 + part, 1), :, cols(x)], own(2), k in DIRECT_IN)
        bx = Gather(m, "x", lambda q, part: b.at[core, pl.ds(2 * part, 2), q // 2, pl.ds(2, 2), :, cols(q)],
                    direct=k in DIRECT_IN)
        passed = {}

        def turn(name, first, second):
            @task((name, k))
            def _():
                if k not in landed:
                    own_copies[k].wait()
                    landed.add(k)
                first.end()
                second.begin()

        def give(name, last, first_row):
            @task((name, k))
            def _():
                last.end()
                view = b.at[core, :, :, pl.ds(first_row, 2)]
                passed[name] = m.start(view, view, core=1 - core)

        for name, ring in (("ax1", ax), ("bz1", bz), ("az1", az), ("bx1", bx)):
            tasks[name + "a", k] = ring.forward_up
            tasks[name + "b", k] = ring.forward_down
        tasks["ax0", k], tasks["bz0", k] = ax.begin, bz.begin
        turn("ax2", ax, az)
        turn("bz2", bz, bx)
        give("az2", az, 0)
        give("bx2", bx, 2)
        return passed

    landed = set()
    passed = [input_tasks(k) for k in CHUNKS]

    def rows_of(part):
        first, end = part
        return pl.ds(STARTS[first], sum(SPANS[first:end]))

    cot_moves = {}

    def cot_tasks(i):
        rows = rows_of(COT_PARTS[i])

        @task(("c0", i))
        def _():
            cot_moves[i] = [m.here(cot_ref.at[y, rows], cot1.at[y, rows])], [
                m.start(cot_ref.at[dev.along("y", s), rows], cot1.at[y, rows], y=dev.along("y", s)) for s in (1, 2, 3)
            ]

        @task(("c1", i))
        def _():
            wait_all(cot_moves[i])

            def source(to):
                return cot1.at[to["z"], rows, pl.ds(pl.multiple_of((to["x"] // 2) * HID, HID), HID)]

            dst = cot.at[z, half, rows]
            cot_moves[i] = [m.here(source(at), dst)], [
                m.start(source(to), dst, **to) for to in (in_plane(*step) for step in plane)
            ]

    def wait_all(moves):
        here, remote = moves
        for copy in here:
            copy.wait()
        for copy in remote:
            copy.wait_recv()

    for i in range(len(COT_PARTS)):
        cot_tasks(i)

    act_moves = {}

    def act_tasks(i):
        rows = rows_of(ACT_PARTS[i])

        @task(("p0", i))
        def _():
            dst = act1.at[z, rows, pl.ds(pl.multiple_of(half * HID, HID), HID)]
            act_moves[i] = [m.here(act.at[z, half, rows], dst)], [
                m.start(act.at[to["z"], to["x"] // 2, rows], dst, **to) for to in (in_plane(*step) for step in plane)
            ]

        @task(("p1", i))
        def _():
            wait_all(act_moves[i])
            act_moves[i] = [m.here(act1.at[y, rows], act_ref.at[y, rows])], [
                m.start(act1.at[dev.along("y", s), rows], act_ref.at[y, rows], y=dev.along("y", s)) for s in (1, 2, 3)
            ]

        @task(("p2", i))
        def _():
            wait_all(act_moves[i])

    for i in range(len(ACT_PARTS)):
        act_tasks(i)

    def main_tasks(k):
        b, p, s, d, near = (bufs[name][k] for name in ("x", "p", "s", "d", "ynear"))
        r, rows = SPANS[k], pl.ds(STARTS[k], SPANS[k])
        total = Reduce(m, "y", lambda q, part: p.at[pl.ds(2 * part, 2), :, q], bufs["yfar"][k], near, add_rows)
        spread = Gather(m, "y", lambda q, part: s.at[pl.ds(2 * part, 2), :, q])
        state = {}

        @task(("P", k))
        def _():
            for copy in passed[k].values():
                copy.wait_recv()
            while w_copies:
                w_copies.pop().wait()

            def tile(n, carry):
                where = pl.ds(pl.multiple_of(n * 256, 256), 256)
                value = jnp.dot(b[0].reshape(32 * r, HID), w[0, :, where], preferred_element_type=F32)
                value += jnp.dot(b[1].reshape(32 * r, HID), w[1, :, where], preferred_element_type=F32)
                p[:, :, :, :, where] = value.astype(BF16).reshape(4, 2, 4, r, 256)
                return carry

            lax.fori_loop(0, 3, tile, 0)
            total.begin()

        tasks["R1a", k], tasks["R1b", k] = total.middle_up, total.middle_down

        @task(("G", k))
        def _():
            total.arrive()
            for i, (first, end) in enumerate(COT_PARTS):
                if first <= k < end and i in cot_moves:
                    wait_all(cot_moves.pop(i))

            def step(i, carry):
                zz, hh = i // 2, i % 2
                value = p[zz, hh, y].astype(F32)
                value = value + near[0, zz // 2, zz % 2, hh].astype(F32) + near[1, zz // 2, zz % 2, hh].astype(F32)
                a, slope = gelu_and_slope(value, cot[zz, hh, rows].astype(F32))
                act[zz, hh, rows] = a.astype(BF16)
                s[zz, hh, y] = slope.astype(BF16)
                return carry

            lax.fori_loop(0, 8, step, 0)
            spread.begin()

        tasks["A1a", k], tasks["A1b", k] = spread.forward_up, spread.forward_down

        def input_terms(c):
            def tile(n, carry):
                where = pl.ds(pl.multiple_of(n * 256, 256), 256)
                value = lax.dot_general(
                    s[...].reshape(32 * r, HID), w[c, where, :], (((1,), (1,)), ((), ())), preferred_element_type=F32
                )
                d[c, :, :, :, :, where] = value.astype(BF16).reshape(4, 2, 4, r, 256)
                return carry

            lax.fori_loop(0, 3, tile, 0)

        @task(("Dh", k))
        def _():
            spread.end()
            input_terms(1 - core)
            state["cross"] = m.start(d.at[1 - core], bufs["core"][k], core=1 - core)

        @task(("Dl", k))
        def _():
            input_terms(core)

        @task(("W", k))
        def _():
            def tile(n, carry):
                c = n // 3
                where = pl.ds(pl.multiple_of((n % 3) * 256, 256), 256)
                value = lax.dot_general(
                    b[c, :, :, :, :, where].reshape(32 * r, 256), s[...].reshape(32 * r, HID),
                    (((0,), (0,)), ((), ())), preferred_element_type=F32,
                )
                if k > 0:
                    value = value + acc[c, where, :]
                if k < last:
                    acc[c, where, :] = value
                else:
                    dw[c, where, :] = value.astype(BF16)
                return carry

            lax.fori_loop(0, 6, tile, 0)
            if k == last:
                for c in range(2):
                    for lo in range(2):
                        outs.append(m.here(dw.at[c, pl.ds(lo * FEAT, FEAT)], dw_ref.at[lo, c]))

        ax = Reduce(m, "x", lambda q, part: d.at[core, pl.ds(2 * part, 2), q // 2, pl.ds(0, 2), :, cols(q)],
                    bufs["axfar"][k], bufs["axnear"][k], add_into, k in DIRECT_OUT)
        bz = Reduce(m, "z", lambda q, part: d.at[core, q, pl.ds(part, 1), pl.ds(2, 2)],
                    bufs["bzfar"][k], bufs["bznear"][k], add_into, k in DIRECT_OUT)
        az = Reduce(m, "z", lambda q, part: d.at[core, q, half, pl.ds(part, 1), :, cols(x)],
                    bufs["azfar"][k], bufs["aznear"][k], add_into, k in DIRECT_OUT)
        bx = Reduce(m, "x", lambda q, part: d.at[core, z, q // 2, pl.ds(2 + part, 1), :, cols(q)],
                    bufs["bxfar"][k], bufs["bxnear"][k], add_into, k in DIRECT_OUT)
        for name, ring in (("rx1", ax), ("rz1", bz), ("sz1", az), ("sx1", bx)):
            tasks[name + "a", k] = ring.middle_up
            tasks[name + "b", k] = ring.middle_down

        @task(("dx0", k))
        def _():
            state["cross"].wait_recv()
            add_rows(d.at[core], bufs["core"][k])
            ax.begin()
            bz.begin()

        @task(("rx2", k))
        def _():
            ax.end()
            az.begin()

        @task(("rz2", k))
        def _():
            bz.end()
            bx.begin()

        @task(("sz2", k))
        def _():
            az.end()
            dx_ref[0:2, rows, :] = d[core, z, half, 0:2, :, cols(x)]

        @task(("sx2", k))
        def _():
            bx.end()
            dx_ref[2:4, rows, :] = d[core, z, half, 2:4, :, cols(x)]

    last, outs = len(SPANS) - 1, []
    for k in CHUNKS:
        main_tasks(k)
    for step in ORDER:
        tasks[step]()
    for copy in outs:
        copy.wait()
    m.drain()


def on_device(inputs, weight, cotangent):
    shapes = [pltpu.VMEM(shape, BF16) for name, each in scratch_of().items() for shape in each]
    act, dx, dw = pl.pallas_call(
        kernel,
        out_shape=(
            jax.ShapeDtypeStruct((4, OWN, 2 * HID), BF16),
            jax.ShapeDtypeStruct((4, OWN, FEAT), BF16),
            jax.ShapeDtypeStruct((2, 2, FEAT, HID), BF16),
        ),
        in_specs=[
            pl.BlockSpec(memory_space=pltpu.VMEM),
            pl.BlockSpec(memory_space=pl.ANY),
            pl.BlockSpec(memory_space=pl.ANY),
        ],
        out_specs=(
            pl.BlockSpec(memory_space=pl.ANY),
            pl.BlockSpec(memory_space=pltpu.VMEM),
            pl.BlockSpec(memory_space=pl.ANY),
        ),
        scratch_shapes=[
            *shapes,
            pltpu.VMEM((2, HID, HID), BF16),
            pltpu.VMEM((2, HID, HID), F32),
            pltpu.VMEM((2, HID, HID), BF16),
            pltpu.VMEM((4, OWN, 2 * HID), BF16),
            pltpu.VMEM((4, 2, OWN, HID), BF16),
            pltpu.VMEM((4, 2, OWN, HID), BF16),
            pltpu.VMEM((4, OWN, 2 * HID), BF16),
            pltpu.SemaphoreType.DMA((N_SEM,)),
            pltpu.SemaphoreType.DMA((N_SEM,)),
            pltpu.SemaphoreType.DMA((N_LOCAL,)),
        ],
        compiler_params=pltpu.CompilerParams(
            collective_id=0, has_side_effects=True, vmem_limit_bytes=62 * 2**20
        ),
        cost_estimate=pl.CostEstimate(flops=6 * 384 * 1536 * 6144, bytes_accessed=8 * 2**20, transcendentals=0),
    )(
        inputs.reshape(4, OWN, FEAT),
        weight.reshape(2, 2, FEAT, HID),
        cotangent.reshape(4, OWN, 2 * HID),
    )
    return act.reshape(4 * OWN, 2 * HID), dx.reshape(4 * OWN, FEAT), dw.reshape(4 * FEAT, HID)


def solution(mesh):
    return jax.shard_map(
        on_device,
        mesh=mesh,
        in_specs=(P("gy", ("gz", "gx")), P("gz", ("gx", "gy")), P("gy", ("gx", "gz"))),
        out_specs=(P("gy", ("gx", "gz")), P("gy", ("gz", "gx")), P("gz", ("gx", "gy"))),
        check_vma=False,
    )
```

time: 618 us -> 140 us (0.23)
  the two profiles are of different devices: /device:TPU:1 before, /device:TPU:25 now
where the time goes in v2:
time: 140 us
  Pallas kernels  134 us (96%)
  local copies, waits for them, and re-layouts  5.62 us (4%)
    pallas_call x1, Pallas kernels, on_device(): pl.pallas_call(kernel, out_shape=(jax.ShapeDtypeStruct((4, OWN, 2 * HID),...  134 us
    unnamed x5, local copies, waits for them, and re-layouts  5.62 us

profile of v2, /device:TPU:25, one launch (start us, length us, event | category | flops | bytes accessed | tf_op | source)
XLA Modules:
  0.0 140.2 jit_solution(7294386256919124710)
XLA Ops:
  0.6 134.0 %shard_map.58 = (bf16[4,96,1536]{2,1,0:T(8,128)(2,1)}, bf16[4,96,384]{2,1,0:T(8,128)(2,1)}, bf16[2,2,384,768]{3,2,1,0:T(8,128)(2,1)}) custom-call(bf16[4,96,384]{2,1,0:T(8,128)(2,1)} %bitcast.11, bf16[2,2,384,768]{3,2,1,0:T(8,128)(2,1)} %bitcast.9, bf16[4,96,1536]{2,1,0:T(8,128)(2,1)} %bitcast.10), custom_call_target="tpu_custom_call" | custom-call | flops 21743271936 | bytes 8388608 | tf_op jit(solution)/shard_map/pallas_call | solution.py:504
  134.6 0.0 copy-start
  134.6 2.5 %copy.9 = bf16[384,1536]{1,0:T(8,128)(2,1)} copy(bf16[384,1536]{1,0:T(8,128)(2,1)} %bitcast.7) | data formatting | bytes 2359296
  137.1 1.7 %copy.10 = bf16[384,384]{1,0:T(8,128)(2,1)} copy(bf16[384,384]{1,0:T(8,128)(2,1)} %bitcast.8) | data formatting | bytes 589824
  138.8 0.0 copy-done
  138.8 1.4 %copy.11 = bf16[1536,768]{1,0:T(8,128)(2,1)} copy(bf16[1536,768]{1,0:T(8,128)(2,1)S(1)} %bitcast.6) | data formatting | bytes 4718592
Async XLA Ops:
  134.6 4.2 %copy-start = (bf16[2,2,384,768]{3,2,1,0:T(8,128)(2,1)S(1)}, bf16[2,2,384,768]{3,2,1,0:T(8,128)(2,1)}, u32[]{:S(2)}) copy-start(bf16[2,2,384,768]{3,2,1,0:T(8,128)(2,1)} %get-tuple-element.8) | copy-start | bytes 7077892

commit v3 on v2

v3 whole, which is shorter than its diff:
```python
import functools

import jax
import jax.numpy as jnp
from jax import lax
from jax.experimental import pallas as pl
from jax.experimental.pallas import tpu as pltpu
from jax.sharding import PartitionSpec as P

MESH = pl.DeviceIdType.MESH
F32, BF16 = jnp.float32, jnp.bfloat16
RING = 4
SPANS = (16, 16, 16, 16, 16, 16)
OWN = sum(SPANS)
STARTS = tuple(sum(SPANS[:k]) for k in range(len(SPANS)))
CHUNKS = range(len(SPANS))
HID = 768
FEAT = 384
COT_PARTS = ((0, 1), (1, 6))
ACT_PARTS = ((0, 5), (5, 6))
N_SEM = 17 * len(SPANS) + 2 * (len(COT_PARTS) + len(ACT_PARTS)) + 2
ORDER = (
    ("bz0", 0), ("c0", 0), ("ax0", 0), ("ax0", 2), ("bz0", 2), ("ax0", 1), ("bz0", 3), ("bz0", 1), ("bz2", 0),
    ("c0", 1), ("ax2", 0), ("ax2", 1), ("bz0", 4), ("bz2", 1), ("ax0", 4), ("ax2", 2), ("ax0", 3), ("bx2", 0),
    ("bz2", 2), ("az2", 0), ("c1", 0), ("P", 0), ("bx2", 1), ("az2", 1), ("P", 1), ("az2", 2), ("bz2", 3),
    ("bz2", 4), ("bz0", 5), ("bx2", 2), ("R1a", 0), ("ax2", 4), ("ax2", 3), ("ax0", 5), ("R1b", 0), ("P", 2),
    ("R1a", 1), ("G", 0), ("bx2", 3), ("c1", 1), ("R1a", 2), ("az2", 4), ("R1b", 1), ("az2", 3), ("bx2", 4),
    ("R1b", 2), ("P", 3), ("P", 4), ("ax2", 5), ("A1b", 0), ("A1a", 0), ("R1a", 3), ("bz2", 5), ("G", 2),
    ("R1b", 4), ("R1a", 4), ("G", 1), ("R1b", 3), ("Dh", 0), ("bx2", 5), ("A1b", 2), ("az2", 5), ("Dl", 0),
    ("dx0", 0), ("P", 5), ("A1a", 2), ("W", 0), ("A1b", 1), ("A1a", 1), ("G", 4), ("G", 3), ("p0", 0),
    ("rx2", 0), ("Dh", 2), ("Dh", 1), ("W", 1), ("R1a", 5), ("R1b", 5), ("Dl", 2), ("dx0", 2), ("rz2", 0),
    ("A1b", 3), ("A1a", 3), ("Dl", 1), ("sz2", 0), ("A1a", 4), ("dx0", 1), ("A1b", 4), ("W", 2), ("G", 5),
    ("p0", 1), ("Dh", 3), ("W", 3), ("Dl", 3), ("dx0", 3), ("A1b", 5), ("A1a", 5), ("p1", 0), ("Dh", 4),
    ("Dl", 4), ("rx2", 1), ("rz2", 1), ("dx0", 4), ("Dh", 5), ("sx2", 0), ("Dl", 5), ("dx0", 5), ("rz2", 3),
    ("p1", 1), ("rx2", 2), ("rx2", 3), ("W", 4), ("rz2", 2), ("rz2", 4), ("W", 5), ("rx2", 4), ("rz2", 5),
    ("rx2", 5), ("sz2", 1), ("p2", 0), ("sz2", 3), ("p2", 1), ("sx2", 1), ("sx2", 3), ("sx2", 4), ("sx2", 2),
    ("sz2", 2), ("sz2", 4), ("sx2", 5), ("sz2", 5),
)


class Device:
    def __init__(self):
        gx, gy, gz = (lax.axis_index(name) for name in ("gx", "gy", "gz"))
        self.core = gx % 2
        self.at = {"x": (gy % 2) * 2 + gx // 2, "y": gz, "z": gy // 2}

    def name(self, core=None, **at):
        at = {**self.at, **at}
        core = self.core if core is None else core
        return {"gx": (at["x"] % 2) * 2 + core, "gy": at["z"] * 2 + at["x"] // 2, "gz": at["y"]}

    def along(self, axis, step):
        return (self.at[axis] + step) % RING


def cols(x):
    return pl.ds(pl.multiple_of((x % 2) * FEAT, FEAT), FEAT)


def gelu_and_slope(value, cotangent):
    scale, cubic = 0.7978845608028654, 0.044715
    square = value * value
    t = jnp.tanh(scale * value * (1.0 + cubic * square))
    half = 0.5 * (1.0 + t)
    slope = half + 0.5 * value * ((1.0 + t) * (1.0 - t)) * (scale + (3.0 * cubic * scale) * square)
    return value * half, cotangent * slope


def add_into(dst, *srcs):
    total = dst[...].astype(F32)
    for src in srcs:
        total = total + src[...].astype(F32)
    dst[...] = total.astype(BF16)


def add_rows(dst, *srcs):
    def step(i, carry):
        add_into(dst.at[i], *(src.at[i] for src in srcs))
        return carry

    lax.fori_loop(0, dst.shape[0], step, 0)


class Moves:
    def __init__(self, device, send, recv):
        self.device, self.send, self.recv = device, send, recv
        self.count = 0
        self.sent = []

    def sem(self):
        self.count += 1
        return self.recv.at[self.count - 1]

    def start(self, src, dst, sem, **to):
        copy = pltpu.make_async_remote_copy(
            src_ref=src, dst_ref=dst, send_sem=self.send, recv_sem=sem,
            device_id=self.device.name(**to), device_id_type=MESH,
        )
        copy.start()
        self.sent.append(copy)

    def here(self, src, dst, sem):
        pltpu.make_async_copy(src, dst, sem).start()

    def wait(self, size, sem):
        pltpu.make_async_copy(size, size, sem).wait()

    def drain(self):
        for copy in self.sent:
            copy.wait_send()
        self.sent = []


class Straight:
    def __init__(self, moves, axis, size):
        self.m, self.axis, self.size, self.sem = moves, axis, size, moves.sem()

    def send(self, src, dst):
        for step in (1, 3, 2):
            to = self.m.device.along(self.axis, step)
            self.m.start(src(to), dst(step), self.sem, **{self.axis: to})

    def arrive(self):
        self.m.wait(self.size, self.sem)


class Gather:
    def __init__(self, moves, axis, slot, rest):
        self.m, self.axis, self.slot, self.rest = moves, axis, slot, rest
        self.up_sem, self.down_sem, self.rest_sem = moves.sem(), moves.sem(), moves.sem()

    def begin(self):
        d, a = self.m.device, self.axis
        me, up, down = d.at[a], {a: d.along(a, 1)}, {a: d.along(a, 3)}
        first, second = self.slot(me, 0), self.slot(me, 1)
        self.m.start(first, first, self.up_sem, **up)
        self.m.start(second, second, self.down_sem, **down)
        self.m.start(second, second, self.rest_sem, **up)
        self.m.start(first, first, self.rest_sem, **down)

    def forward_up(self):
        d, a = self.m.device, self.axis
        view = self.slot(d.along(a, 3), 0)
        self.m.wait(view, self.up_sem)
        self.m.start(view, view, self.rest_sem, **{a: d.along(a, 1)})

    def forward_down(self):
        d, a = self.m.device, self.axis
        view = self.slot(d.along(a, 1), 1)
        self.m.wait(view, self.down_sem)
        self.m.start(view, view, self.rest_sem, **{a: d.along(a, 3)})

    def end(self):
        self.m.wait(self.rest, self.rest_sem)


class Reduce:
    def __init__(self, moves, axis, piece, far, near):
        self.m, self.axis, self.piece, self.far, self.near = moves, axis, piece, far, near
        self.up_sem, self.down_sem, self.near_sem = moves.sem(), moves.sem(), moves.sem()

    def begin(self):
        d, a, p = self.m.device, self.axis, self.piece
        up, down, across = d.along(a, 1), d.along(a, 3), d.along(a, 2)
        self.m.start(p(across, 0), self.far.at[0], self.up_sem, **{a: up})
        self.m.start(p(across, 1), self.far.at[1], self.down_sem, **{a: down})
        self.m.start(p(up, 1), self.near.at[0, 1], self.near_sem, **{a: up})
        self.m.start(p(down, 0), self.near.at[1, 0], self.near_sem, **{a: down})

    def middle_up(self):
        d, a = self.m.device, self.axis
        up = d.along(a, 1)
        self.m.wait(self.far.at[0], self.up_sem)
        add_rows(self.piece(up, 0), self.far.at[0])
        self.m.start(self.piece(up, 0), self.near.at[0, 0], self.near_sem, **{a: up})

    def middle_down(self):
        d, a = self.m.device, self.axis
        down = d.along(a, 3)
        self.m.wait(self.far.at[1], self.down_sem)
        add_rows(self.piece(down, 1), self.far.at[1])
        self.m.start(self.piece(down, 1), self.near.at[1, 1], self.near_sem, **{a: down})

    def arrive(self):
        self.m.wait(self.near, self.near_sem)


def scratch_of():
    shapes = {}
    for k in CHUNKS:
        r = SPANS[k]
        block = (4, 2, 4, r, HID)
        for name, shape in dict(
            x=(2, *block), p=block, s=block, d=(2, *block), core=block,
            yfar=(2, 2, 2, r, HID), ynear=(2, 2, 2, 2, r, HID),
            ax=(3, 4, 2, r, FEAT), az=(3, 2, r, FEAT), bz=(3, 2, 2, r, HID), bx=(3, 2, r, FEAT),
        ).items():
            shapes.setdefault(name, []).append(shape)
    return shapes


NAMES = tuple(scratch_of())


def kernel(in_ref, w_ref, cot_ref, act_ref, dx_ref, dw_ref, *scratch):
    bufs, rest = {}, list(scratch)
    for name in NAMES:
        bufs[name] = [rest.pop(0) for _ in CHUNKS]
    w, acc, cot1, cot, act, act1, send, recv = rest
    dev = Device()
    core, at = dev.core, dev.at
    x, y, z = at["x"], at["y"], at["z"]
    half = x // 2
    m = Moves(dev, send, recv)
    plane = [(dz, dh) for dz in range(4) for dh in range(2) if (dz, dh) != (0, 0)]

    def in_plane(dz, dh):
        return dict(z=(z + dz) % RING, x=((half + dh) % 2) * 2 + x % 2)

    w_sem, own_sems = m.sem(), [m.sem() for _ in CHUNKS]
    for c in range(2):
        for lo in range(2):
            m.here(w_ref.at[lo, c], w.at[c, pl.ds(lo * FEAT, FEAT)], w_sem)
    own_blocks = [bufs["x"][k].at[core, z, half, :, :, cols(x)] for k in CHUNKS]
    for k in CHUNKS:
        m.here(in_ref.at[:, pl.ds(STARTS[k], SPANS[k])], own_blocks[k], own_sems[k])

    barrier = pltpu.get_barrier_semaphore()
    peers = [dict(core=1 - core), dict(x=dev.along("x", 1)), dict(x=dev.along("x", 3))]
    peers += [dict(y=dev.along("y", s)) for s in (1, 2, 3)] + [in_plane(*step) for step in plane if 0 in step]
    for peer in peers:
        pl.semaphore_signal(barrier, inc=1, device_id=dev.name(**peer), device_id_type=MESH)
    pl.semaphore_wait(barrier, len(peers))

    tasks = {}

    def task(name):
        def keep(step):
            tasks[name] = step
            return step

        return keep

    landed, core_sems = set(), []

    def input_tasks(k):
        b = bufs["x"][k]
        rows = pl.ds(STARTS[k], SPANS[k])

        ax = Straight(m, "x", b.at[core, pl.ds(0, 3), 0, pl.ds(0, 2), :, pl.ds(0, FEAT)])
        az = Straight(m, "z", b.at[core, pl.ds(0, 3), :, pl.ds(0, 2)])
        bz = Straight(m, "z", b.at[core, pl.ds(0, 3), 0, pl.ds(0, 2), :, pl.ds(0, FEAT)])
        bx = Straight(m, "x", b.at[core, pl.ds(0, 3), 0])
        core_sems.append(m.sem())

        @task(("ax0", k))
        def _():
            ax.send(lambda to: in_ref.at[0:2, rows], lambda step: b.at[core, z, half, 0:2, :, cols(x)])

        @task(("bz0", k))
        def _():
            bz.send(lambda to: in_ref.at[2:4, rows], lambda step: b.at[core, z, half, 2:4, :, cols(x)])

        def own_landed():
            if k not in landed:
                m.wait(own_blocks[k], own_sems[k])
                landed.add(k)

        @task(("ax2", k))
        def _():
            own_landed()
            ax.arrive()
            view = b.at[core, z, :, 0:2]
            az.send(lambda to: view, lambda step: view)

        @task(("bz2", k))
        def _():
            own_landed()
            bz.arrive()
            view = b.at[core, :, half, 2:4, :, cols(x)]
            bx.send(lambda to: view, lambda step: view)

        def give(ring, first_row):
            ring.arrive()
            view = b.at[core, :, :, pl.ds(first_row, 2)]
            m.start(view, view, core_sems[k], core=1 - core)

        tasks["az2", k] = lambda: give(az, 0)
        tasks["bx2", k] = lambda: give(bx, 2)

    for k in CHUNKS:
        input_tasks(k)

    def rows_of(part):
        first, end = part
        return pl.ds(STARTS[first], sum(SPANS[first:end]))

    def cot_tasks(i):
        rows, y_sem, plane_sem = rows_of(COT_PARTS[i]), m.sem(), m.sem()

        @task(("c0", i))
        def _():
            m.here(cot_ref.at[y, rows], cot1.at[y, rows], y_sem)
            for s in (1, 2, 3):
                to = dev.along("y", s)
                m.start(cot_ref.at[to, rows], cot1.at[y, rows], y_sem, y=to)

        @task(("c1", i))
        def _():
            m.wait(cot1.at[:, rows], y_sem)

            def source(to):
                return cot1.at[to["z"], rows, pl.ds(pl.multiple_of((to["x"] // 2) * HID, HID), HID)]

            dst = cot.at[z, half, rows]
            m.here(source(at), dst, plane_sem)
            for to in others:
                m.start(source(to), dst, plane_sem, **to)

        def landed():
            m.wait(cot.at[:, :, rows], plane_sem)

        return landed

    others = [in_plane(*step) for step in plane]
    cot_landed = [cot_tasks(i) for i in range(len(COT_PARTS))]

    def act_tasks(i):
        rows, plane_sem, y_sem = rows_of(ACT_PARTS[i]), m.sem(), m.sem()

        @task(("p0", i))
        def _():
            dst = act1.at[z, rows, pl.ds(pl.multiple_of(half * HID, HID), HID)]
            m.here(act.at[z, half, rows], dst, plane_sem)
            for to in others:
                m.start(act.at[to["z"], to["x"] // 2, rows], dst, plane_sem, **to)

        @task(("p1", i))
        def _():
            m.wait(act1.at[:, rows], plane_sem)
            m.here(act1.at[y, rows], act_ref.at[y, rows], y_sem)
            for s in (1, 2, 3):
                to = dev.along("y", s)
                m.start(act1.at[to, rows], act_ref.at[y, rows], y_sem, y=to)

        tasks["p2", i] = lambda: m.wait(act_ref.at[:, rows], y_sem)

    for i in range(len(ACT_PARTS)):
        act_tasks(i)

    def main_tasks(k):
        b, p, s, d, near = (bufs[name][k] for name in ("x", "p", "s", "d", "ynear"))
        r, rows = SPANS[k], pl.ds(STARTS[k], SPANS[k])
        total = Reduce(m, "y", lambda q, part: p.at[pl.ds(2 * part, 2), :, q], bufs["yfar"][k], near)
        spread = Gather(m, "y", lambda q, part: s.at[pl.ds(2 * part, 2), :, q], s.at[:, :, 0:2])
        cross_sem = m.sem()

        @task(("P", k))
        def _():
            m.wait(b.at[1 - core], core_sems[k])
            if "w" not in landed:
                m.wait(w, w_sem)
                landed.add("w")

            def tile(n, carry):
                where = pl.ds(pl.multiple_of(n * 256, 256), 256)
                value = jnp.dot(b[0].reshape(32 * r, HID), w[0, :, where], preferred_element_type=F32)
                value += jnp.dot(b[1].reshape(32 * r, HID), w[1, :, where], preferred_element_type=F32)
                p[:, :, :, :, where] = value.astype(BF16).reshape(4, 2, 4, r, 256)
                return carry

            lax.fori_loop(0, 3, tile, 0)
            total.begin()

        tasks["R1a", k], tasks["R1b", k] = total.middle_up, total.middle_down

        @task(("G", k))
        def _():
            total.arrive()
            for i, (first, end) in enumerate(COT_PARTS):
                if first <= k < end and ("cot", i) not in landed:
                    cot_landed[i]()
                    landed.add(("cot", i))

            def step(i, carry):
                zz, hh = i // 2, i % 2
                value = p[zz, hh, y].astype(F32)
                value = value + near[0, zz // 2, zz % 2, hh].astype(F32) + near[1, zz // 2, zz % 2, hh].astype(F32)
                a, slope = gelu_and_slope(value, cot[zz, hh, rows].astype(F32))
                act[zz, hh, rows] = a.astype(BF16)
                s[zz, hh, y] = slope.astype(BF16)
                return carry

            lax.fori_loop(0, 8, step, 0)
            spread.begin()

        tasks["A1a", k], tasks["A1b", k] = spread.forward_up, spread.forward_down

        def input_terms(c):
            def tile(n, carry):
                where = pl.ds(pl.multiple_of(n * 256, 256), 256)
                value = lax.dot_general(
                    s[...].reshape(32 * r, HID), w[c, where, :], (((1,), (1,)), ((), ())), preferred_element_type=F32
                )
                d[c, :, :, :, :, where] = value.astype(BF16).reshape(4, 2, 4, r, 256)
                return carry

            lax.fori_loop(0, 3, tile, 0)

        @task(("Dh", k))
        def _():
            spread.end()
            input_terms(1 - core)
            m.start(d.at[1 - core], bufs["core"][k], cross_sem, core=1 - core)

        @task(("Dl", k))
        def _():
            input_terms(core)

        @task(("W", k))
        def _():
            def tile(n, carry):
                c = n // 3
                where = pl.ds(pl.multiple_of((n % 3) * 256, 256), 256)
                value = lax.dot_general(
                    b[c, :, :, :, :, where].reshape(32 * r, 256), s[...].reshape(32 * r, HID),
                    (((0,), (0,)), ((), ())), preferred_element_type=F32,
                )
                if k > 0:
                    value = value + acc[c, where, :]
                if k < last:
                    acc[c, where, :] = value
                else:
                    dw_ref[c, where, :] = value.astype(BF16)
                return carry

            lax.fori_loop(0, 6, tile, 0)

        ax, az, bz, bx = (Straight(m, axis, bufs[name][k]) for name, axis in (("ax", "x"), ("az", "z"), ("bz", "z"), ("bx", "x")))
        land = {name: bufs[name][k] for name in ("ax", "az", "bz", "bx")}

        def pieces(name):
            return {
                "ax": lambda q: d.at[core, :, q // 2, 0:2, :, cols(q)],
                "bz": lambda q: d.at[core, q, :, 2:4],
                "az": lambda q: d.at[core, q, half, 0:2, :, cols(x)],
                "bx": lambda q: d.at[core, z, q // 2, 2:4, :, cols(q)],
            }[name]

        def send(ring, name):
            ring.send(pieces(name), lambda step: land[name].at[step - 1])

        def finish(ring, name):
            ring.arrive()
            add_rows(pieces(name)(at[ring.axis]), *(land[name].at[i] for i in range(3)))

        @task(("dx0", k))
        def _():
            m.wait(bufs["core"][k], cross_sem)
            add_rows(d.at[core], bufs["core"][k])
            send(ax, "ax")
            send(bz, "bz")

        @task(("rx2", k))
        def _():
            finish(ax, "ax")
            send(az, "az")

        @task(("rz2", k))
        def _():
            finish(bz, "bz")
            send(bx, "bx")

        @task(("sz2", k))
        def _():
            finish(az, "az")
            dx_ref[0:2, rows, :] = d[core, z, half, 0:2, :, cols(x)]

        @task(("sx2", k))
        def _():
            finish(bx, "bx")
            dx_ref[2:4, rows, :] = d[core, z, half, 2:4, :, cols(x)]

    last = len(SPANS) - 1
    for k in CHUNKS:
        main_tasks(k)
    for step in ORDER:
        tasks[step]()
    m.drain()


def on_device(inputs, weight, cotangent):
    shapes = [pltpu.VMEM(shape, BF16) for name, each in scratch_of().items() for shape in each]
    act, dx, dw = pl.pallas_call(
        kernel,
        out_shape=(
            pltpu.VMEM((4, OWN, 2 * HID), BF16),
            pltpu.VMEM((4, OWN, FEAT), BF16),
            pltpu.VMEM((2, HID, HID), BF16),
        ),
        in_specs=[
            pl.BlockSpec(memory_space=pltpu.VMEM),
            pl.BlockSpec(memory_space=pl.ANY),
            pl.BlockSpec(memory_space=pl.ANY),
        ],
        out_specs=(
            pl.BlockSpec(memory_space=pltpu.VMEM),
            pl.BlockSpec(memory_space=pltpu.VMEM),
            pl.BlockSpec(memory_space=pltpu.VMEM),
        ),
        scratch_shapes=[
            *shapes,
            pltpu.VMEM((2, HID, HID), BF16),
            pltpu.VMEM((2, HID, HID), F32),
            pltpu.VMEM((4, OWN, 2 * HID), BF16),
            pltpu.VMEM((4, 2, OWN, HID), BF16),
            pltpu.VMEM((4, 2, OWN, HID), BF16),
            pltpu.VMEM((4, OWN, 2 * HID), BF16),
            pltpu.SemaphoreType.DMA,
            pltpu.SemaphoreType.DMA((N_SEM,)),
        ],
        compiler_params=pltpu.CompilerParams(
            collective_id=0, has_side_effects=True, vmem_limit_bytes=58 * 2**20
        ),
        cost_estimate=pl.CostEstimate(flops=6 * 384 * 1536 * 6144, bytes_accessed=8 * 2**20, transcendentals=0),
    )(
        inputs.reshape(4, OWN, FEAT),
        weight.reshape(2, 2, FEAT, HID),
        cotangent.reshape(4, OWN, 2 * HID),
    )

    def write_out(act_ref, dx_ref, dw_ref, act_out, dx_out, dw_out, sems):
        pairs = [(act_ref, act_out), (dx_ref, dx_out)]
        pairs += [(dw_ref.at[c, pl.ds(lo * FEAT, FEAT)], dw_out.at[lo, c]) for c in range(2) for lo in range(2)]
        copies = [pltpu.make_async_copy(src, dst, sems.at[i]) for i, (src, dst) in enumerate(pairs)]
        for copy in copies:
            copy.start()
        for copy in copies:
            copy.wait()

    act, dx, dw = pl.pallas_call(
        write_out,
        out_shape=(
            jax.ShapeDtypeStruct((4, OWN, 2 * HID), BF16),
            jax.ShapeDtypeStruct((4, OWN, FEAT), BF16),
            jax.ShapeDtypeStruct((2, 2, FEAT, HID), BF16),
        ),
        in_specs=[pl.BlockSpec(memory_space=pl.ANY)] * 3,
        out_specs=(pl.BlockSpec(memory_space=pl.ANY),) * 3,
        scratch_shapes=[pltpu.SemaphoreType.DMA((6,))],
        compiler_params=pltpu.CompilerParams(vmem_limit_bytes=2**20),
    )(act, dx, dw)
    return act.reshape(4 * OWN, 2 * HID), dx.reshape(4 * OWN, FEAT), dw.reshape(4 * FEAT, HID)


def solution(mesh):
    return jax.shard_map(
        on_device,
        mesh=mesh,
        in_specs=(P("gy", ("gz", "gx")), P("gz", ("gx", "gy")), P("gy", ("gx", "gz"))),
        out_specs=(P("gy", ("gx", "gz")), P("gy", ("gz", "gx")), P("gz", ("gx", "gy"))),
        check_vma=False,
    )
```

time: 140 us -> 126 us (0.900)
  Pallas kernels: 134 us -> 125 us
  local copies, waits for them, and re-layouts: 5.62 us -> 0 us
    pallas_call x1 -> x2, Pallas kernels: 134 us -> 125 us  [the longest x1 123 us: on_device(): pl.pallas_call(kernel, out_shape=(pltpu.VMEM((4, OWN, 2 * HID), BF16), pl...]
    unnamed x5 -> x0, local copies, waits for them, and re-layouts: 5.62 us -> none
where the time goes in v3:
time: 126 us
  Pallas kernels  125 us (99%)
    pallas_call x1, Pallas kernels, on_device(): pl.pallas_call(kernel, out_shape=(pltpu.VMEM((4, OWN, 2 * HID), BF16), pl...  123 us

profile of v3, /device:TPU:25, one launch (start us, length us, event | category | flops | bytes accessed | tf_op | source)
XLA Modules:
  0.0 126.1 jit_solution(8692333783551268253)
XLA Ops:
  0.6 123.5 %shard_map.58 = (bf16[4,96,1536]{2,1,0:T(8,128)(2,1)S(1)}, bf16[4,96,384]{2,1,0:T(8,128)(2,1)S(1)}, bf16[2,768,768]{2,1,0:T(8,128)(2,1)S(1)}) custom-call(bf16[4,96,384]{2,1,0:T(8,128)(2,1)} %bitcast.10, bf16[2,2,384,768]{3,2,1,0:T(8,128)(2,1)} %bitcast.6, bf16[4,96,1536]{2,1,0:T(8,128)(2,1)} %bitcast.8), custom_call_target="tpu_custom_call" | custom-call | flops 21743271936 | bytes 8388608 | tf_op jit(solution)/shard_map/pallas_call | solution.py:494
  124.1 1.9 %shard_map.59 = (bf16[4,96,1536]{2,1,0:T(8,128)(2,1)}, bf16[4,96,384]{2,1,0:T(8,128)(2,1)}, bf16[2,2,384,768]{3,2,1,0:T(8,128)(2,1)}) custom-call(bf16[4,96,1536]{2,1,0:T(8,128)(2,1)S(1)} %get-tuple-element.9.act_ref, bf16[4,96,384]{2,1,0:T(8,128)(2,1)S(1)} %get-tuple-element.10.dx_ref, bf16[2,768,768]{2,1,0:T(8,128)(2,1)S(1)} %get-tuple-element.11.dw_ref), custom_call_target="tpu_custom_call" | custom-call | tf_op jit(solution)/shard_map/pallas_call | solution.py:541

commit v4 on v3

--- a/solution.py
+++ b/solution.py
@@ -362,14 +362,9 @@
                 m.wait(w, w_sem)
                 landed.add("w")
 
-            def tile(n, carry):
-                where = pl.ds(pl.multiple_of(n * 256, 256), 256)
-                value = jnp.dot(b[0].reshape(32 * r, HID), w[0, :, where], preferred_element_type=F32)
-                value += jnp.dot(b[1].reshape(32 * r, HID), w[1, :, where], preferred_element_type=F32)
-                p[:, :, :, :, where] = value.astype(BF16).reshape(4, 2, 4, r, 256)
-                return carry
-
-            lax.fori_loop(0, 3, tile, 0)
+            value = jnp.dot(b[0].reshape(32 * r, HID), w[0], preferred_element_type=F32)
+            value += jnp.dot(b[1].reshape(32 * r, HID), w[1], preferred_element_type=F32)
+            p[...] = value.astype(BF16).reshape(4, 2, 4, r, HID)
             total.begin()
 
         tasks["R1a", k], tasks["R1b", k] = total.middle_up, total.middle_down
@@ -397,15 +392,10 @@
         tasks["A1a", k], tasks["A1b", k] = spread.forward_up, spread.forward_down
 
         def input_terms(c):
-            def tile(n, carry):
-                where = pl.ds(pl.multiple_of(n * 256, 256), 256)
-                value = lax.dot_general(
-                    s[...].reshape(32 * r, HID), w[c, where, :], (((1,), (1,)), ((), ())), preferred_element_type=F32
-                )
-                d[c, :, :, :, :, where] = value.astype(BF16).reshape(4, 2, 4, r, 256)
-                return carry
-
-            lax.fori_loop(0, 3, tile, 0)
+            value = lax.dot_general(
+                s[...].reshape(32 * r, HID), w[c], (((1,), (1,)), ((), ())), preferred_element_type=F32
+            )
+            d[c] = value.astype(BF16).reshape(4, 2, 4, r, HID)
 
         @task(("Dh", k))
         def _():
@@ -419,22 +409,20 @@
 
         @task(("W", k))
         def _():
-            def tile(n, carry):
-                c = n // 3
-                where = pl.ds(pl.multiple_of((n % 3) * 256, 256), 256)
+            def tile(c, carry):
                 value = lax.dot_general(
-                    b[c, :, :, :, :, where].reshape(32 * r, 256), s[...].reshape(32 * r, HID),
+                    b[c].reshape(32 * r, HID), s[...].reshape(32 * r, HID),
                     (((0,), (0,)), ((), ())), preferred_element_type=F32,
                 )
                 if k > 0:
-                    value = value + acc[c, where, :]
+                    value = value + acc[c]
                 if k < last:
-                    acc[c, where, :] = value
+                    acc[c] = value
                 else:
-                    dw_ref[c, where, :] = value.astype(BF16)
+                    dw_ref[c] = value.astype(BF16)
                 return carry
 
-            lax.fori_loop(0, 6, tile, 0)
+            lax.fori_loop(0, 2, tile, 0)
 
         ax, az, bz, bx = (Straight(m, axis, bufs[name][k]) for name, axis in (("ax", "x"), ("az", "z"), ("bz", "z"), ("bx", "x")))
         land = {name: bufs[name][k] for name in ("ax", "az", "bz", "bx")}

time: 126 us -> 122 us (0.968)
  the two profiles are of different devices: /device:TPU:25 before, /device:TPU:1 now
where the time goes in v4:
time: 122 us
  Pallas kernels  122 us (100%)
    pallas_call x1, Pallas kernels, on_device(): pl.pallas_call(kernel, out_shape=(pltpu.VMEM((4, OWN, 2 * HID), BF16), pl...  120 us

profile of v4, /device:TPU:1, one launch (start us, length us, event | category | flops | bytes accessed | tf_op | source)
XLA Modules:
  0.0 122.3 jit_solution(13573396891563611587)
XLA Ops:
  0.6 119.6 %shard_map.58 = (bf16[4,96,1536]{2,1,0:T(8,128)(2,1)S(1)}, bf16[4,96,384]{2,1,0:T(8,128)(2,1)S(1)}, bf16[2,768,768]{2,1,0:T(8,128)(2,1)S(1)}) custom-call(bf16[4,96,384]{2,1,0:T(8,128)(2,1)} %bitcast.10, bf16[2,2,384,768]{3,2,1,0:T(8,128)(2,1)} %bitcast.6, bf16[4,96,1536]{2,1,0:T(8,128)(2,1)} %bitcast.8), custom_call_target="tpu_custom_call" | custom-call | flops 21743271936 | bytes 8388608 | tf_op jit(solution)/shard_map/pallas_call | solution.py:482
  120.2 1.9 %shard_map.59 = (bf16[4,96,1536]{2,1,0:T(8,128)(2,1)}, bf16[4,96,384]{2,1,0:T(8,128)(2,1)}, bf16[2,2,384,768]{3,2,1,0:T(8,128)(2,1)}) custom-call(bf16[4,96,1536]{2,1,0:T(8,128)(2,1)S(1)} %get-tuple-element.9.act_ref, bf16[4,96,384]{2,1,0:T(8,128)(2,1)S(1)} %get-tuple-element.10.dx_ref, bf16[2,768,768]{2,1,0:T(8,128)(2,1)S(1)} %get-tuple-element.11.dw_ref), custom_call_target="tpu_custom_call" | custom-call | tf_op jit(solution)/shard_map/pallas_call | solution.py:529

commit v5 on v4

--- a/solution.py
+++ b/solution.py
@@ -10,6 +10,7 @@
 MESH = pl.DeviceIdType.MESH
 F32, BF16 = jnp.float32, jnp.bfloat16
 RING = 4
+STEPS = {1: "u", 3: "d", 2: "a"}
 SPANS = (16, 16, 16, 16, 16, 16)
 OWN = sum(SPANS)
 STARTS = tuple(sum(SPANS[:k]) for k in range(len(SPANS)))
@@ -17,24 +18,28 @@
 HID = 768
 FEAT = 384
 COT_PARTS = ((0, 1), (1, 6))
-ACT_PARTS = ((0, 5), (5, 6))
-N_SEM = 17 * len(SPANS) + 2 * (len(COT_PARTS) + len(ACT_PARTS)) + 2
+ACT_PARTS = ((0, 3), (3, 5), (5, 6))
+EAGER_IN = (0,)
+EAGER_OUT = (5,)
+N_SEM = 17 * len(SPANS) + 2 * (len(COT_PARTS) + len(ACT_PARTS)) + 2 + 6 * len(EAGER_IN) + 8 * len(EAGER_OUT)
 ORDER = (
-    ("bz0", 0), ("c0", 0), ("ax0", 0), ("ax0", 2), ("bz0", 2), ("ax0", 1), ("bz0", 3), ("bz0", 1), ("bz2", 0),
-    ("c0", 1), ("ax2", 0), ("ax2", 1), ("bz0", 4), ("bz2", 1), ("ax0", 4), ("ax2", 2), ("ax0", 3), ("bx2", 0),
-    ("bz2", 2), ("az2", 0), ("c1", 0), ("P", 0), ("bx2", 1), ("az2", 1), ("P", 1), ("az2", 2), ("bz2", 3),
-    ("bz2", 4), ("bz0", 5), ("bx2", 2), ("R1a", 0), ("ax2", 4), ("ax2", 3), ("ax0", 5), ("R1b", 0), ("P", 2),
-    ("R1a", 1), ("G", 0), ("bx2", 3), ("c1", 1), ("R1a", 2), ("az2", 4), ("R1b", 1), ("az2", 3), ("bx2", 4),
-    ("R1b", 2), ("P", 3), ("P", 4), ("ax2", 5), ("A1b", 0), ("A1a", 0), ("R1a", 3), ("bz2", 5), ("G", 2),
-    ("R1b", 4), ("R1a", 4), ("G", 1), ("R1b", 3), ("Dh", 0), ("bx2", 5), ("A1b", 2), ("az2", 5), ("Dl", 0),
-    ("dx0", 0), ("P", 5), ("A1a", 2), ("W", 0), ("A1b", 1), ("A1a", 1), ("G", 4), ("G", 3), ("p0", 0),
-    ("rx2", 0), ("Dh", 2), ("Dh", 1), ("W", 1), ("R1a", 5), ("R1b", 5), ("Dl", 2), ("dx0", 2), ("rz2", 0),
-    ("A1b", 3), ("A1a", 3), ("Dl", 1), ("sz2", 0), ("A1a", 4), ("dx0", 1), ("A1b", 4), ("W", 2), ("G", 5),
-    ("p0", 1), ("Dh", 3), ("W", 3), ("Dl", 3), ("dx0", 3), ("A1b", 5), ("A1a", 5), ("p1", 0), ("Dh", 4),
-    ("Dl", 4), ("rx2", 1), ("rz2", 1), ("dx0", 4), ("Dh", 5), ("sx2", 0), ("Dl", 5), ("dx0", 5), ("rz2", 3),
-    ("p1", 1), ("rx2", 2), ("rx2", 3), ("W", 4), ("rz2", 2), ("rz2", 4), ("W", 5), ("rx2", 4), ("rz2", 5),
-    ("rx2", 5), ("sz2", 1), ("p2", 0), ("sz2", 3), ("p2", 1), ("sx2", 1), ("sx2", 3), ("sx2", 4), ("sx2", 2),
-    ("sz2", 2), ("sz2", 4), ("sx2", 5), ("sz2", 5),
+    ("ax0", 0), ("bz0", 0), ("c0", 0), ("bz0", 2), ("ax0", 2), ("ax2u", 0), ("c0", 1), ("bz2d", 0),
+    ("ax2a", 0), ("bz2u", 0), ("bz2a", 0), ("ax2d", 0), ("bz0", 4), ("bz2", 2), ("bz0", 3), ("ax0", 4),
+    ("bz0", 1), ("ax2", 2), ("ax0", 1), ("az2", 0), ("ax0", 3), ("ax0", 5), ("bx2", 0), ("P", 0), ("c1", 0),
+    ("bz0", 5), ("bx2", 2), ("bz2", 3), ("az2", 2), ("ax2", 3), ("bz2", 1), ("ax2", 1), ("bz2", 4),
+    ("R1a", 0), ("R1b", 0), ("P", 2), ("G", 0), ("ax2", 4), ("bx2", 3), ("R1a", 2), ("az2", 3), ("R1b", 2),
+    ("P", 3), ("c1", 1), ("bx2", 1), ("az2", 1), ("ax2", 5), ("A1a", 0), ("bx2", 4), ("A1b", 0), ("az2", 4),
+    ("P", 1), ("P", 4), ("Dh", 0), ("R1a", 1), ("R1b", 1), ("bz2", 5), ("G", 2), ("G", 1), ("A1b", 2),
+    ("az2", 5), ("R1b", 3), ("Dl", 0), ("R1a", 3), ("dx0", 0), ("p0", 0), ("A1a", 2), ("A1a", 1), ("W", 0),
+    ("bx2", 5), ("R1a", 4), ("A1b", 1), ("R1b", 4), ("P", 5), ("Dh", 2), ("Dh", 1), ("rz2", 0), ("G", 4),
+    ("Dl", 1), ("dx0", 1), ("R1b", 5), ("G", 3), ("A1b", 4), ("p0", 1), ("Dl", 2), ("R1a", 5), ("W", 1),
+    ("dx0", 2), ("rx2", 0), ("A1a", 4), ("A1b", 3), ("A1a", 3), ("W", 2), ("G", 5), ("rz2", 1), ("sx2", 0),
+    ("p0", 2), ("Dh", 4), ("rz2", 2), ("rx2", 1), ("rx2", 2), ("Dl", 4), ("dx0", 4), ("A1a", 5), ("A1b", 5),
+    ("p1", 1), ("Dh", 3), ("sx2", 2), ("sz2", 1), ("Dl", 3), ("dx0", 3), ("Dh", 5), ("p1", 2), ("sz2", 2),
+    ("p1", 0), ("Dl", 5), ("dx0", 5), ("W", 3), ("W", 4), ("rx2", 3), ("rz2", 4), ("rx2", 4), ("p2", 2),
+    ("rz2", 3), ("rx2a", 5), ("rz2a", 5), ("rz2u", 5), ("sx2", 1), ("rx2u", 5), ("rx2d", 5), ("p2", 1),
+    ("sz2", 0), ("rz2d", 5), ("W", 5), ("sx2", 4), ("p2", 0), ("sz2", 3), ("sx2", 3), ("sz2", 4), ("sz2", 5),
+    ("sx2", 5),
 )
 
 
@@ -115,10 +120,10 @@
     def __init__(self, moves, axis, size):
         self.m, self.axis, self.size, self.sem = moves, axis, size, moves.sem()
 
-    def send(self, src, dst):
-        for step in (1, 3, 2):
+    def send(self, src, dst, sems=None):
+        for step in STEPS:
             to = self.m.device.along(self.axis, step)
-            self.m.start(src(to), dst(step), self.sem, **{self.axis: to})
+            self.m.start(src(to), dst(step), sems[step] if sems else self.sem, **{self.axis: to})
 
     def arrive(self):
         self.m.wait(self.size, self.sem)
@@ -253,13 +258,38 @@
         bx = Straight(m, "x", b.at[core, pl.ds(0, 3), 0])
         core_sems.append(m.sem())
 
+        eager = k in EAGER_IN
+        ax_sems, bz_sems = ({step: m.sem() for step in STEPS} if eager else None for _ in range(2))
+
         @task(("ax0", k))
         def _():
-            ax.send(lambda to: in_ref.at[0:2, rows], lambda step: b.at[core, z, half, 0:2, :, cols(x)])
+            ax.send(lambda to: in_ref.at[0:2, rows], lambda step: b.at[core, z, half, 0:2, :, cols(x)], ax_sems)
+            if eager:
+                az.send(lambda to: in_ref.at[0:2, rows], lambda step: b.at[core, z, half, 0:2, :, cols(x)])
 
         @task(("bz0", k))
         def _():
-            bz.send(lambda to: in_ref.at[2:4, rows], lambda step: b.at[core, z, half, 2:4, :, cols(x)])
+            bz.send(lambda to: in_ref.at[2:4, rows], lambda step: b.at[core, z, half, 2:4, :, cols(x)], bz_sems)
+            if eager:
+                bx.send(lambda to: in_ref.at[2:4, rows], lambda step: b.at[core, z, half, 2:4, :, cols(x)])
+
+        def pass_on(step):
+            @task(("ax2" + STEPS[step], k))
+            def _():
+                q = dev.along("x", RING - step)
+                view = b.at[core, z, q // 2, 0:2, :, cols(q)]
+                m.wait(view, ax_sems[step])
+                az.send(lambda to: view, lambda _: view)
+
+            @task(("bz2" + STEPS[step], k))
+            def _():
+                view = b.at[core, dev.along("z", RING - step), half, 2:4, :, cols(x)]
+                m.wait(view, bz_sems[step])
+                bx.send(lambda to: view, lambda _: view)
+
+        if eager:
+            for step in STEPS:
+                pass_on(step)
 
         def own_landed():
             if k not in landed:
@@ -281,6 +311,7 @@
             bx.send(lambda to: view, lambda step: view)
 
         def give(ring, first_row):
+            own_landed()
             ring.arrive()
             view = b.at[core, :, :, pl.ds(first_row, 2)]
             m.start(view, view, core_sems[k], core=1 - core)
@@ -442,10 +473,57 @@
             ring.arrive()
             add_rows(pieces(name)(at[ring.axis]), *(land[name].at[i] for i in range(3)))
 
+        def x_piece(zz, xx):
+            return d.at[core, zz, xx // 2, 0:2, :, cols(xx)]
+
+        def z_piece(zz, xx):
+            return d.at[core, zz, xx // 2, 2:4, :, cols(xx)]
+
+        def z_land(i, xx):
+            return land["bz"].at[i, xx // 2, :, :, cols(xx)]
+
+        if k in EAGER_OUT:
+            x_sems, z_sems = ([m.sem() for _ in range(RING)] for _ in range(2))
+
+        def sum_x(zz, step, *more):
+            m.wait(land["ax"].at[:, zz], x_sems[step])
+            add_rows(x_piece(zz, x), *(land["ax"].at[i, zz] for i in range(3)), *more)
+
+        def sum_z(xx, step, *more):
+            m.wait(z_land(pl.ds(0, 3), xx), z_sems[step])
+            add_rows(z_piece(z, xx), *(z_land(i, xx) for i in range(3)), *more)
+
+        def pass_on(step):
+            @task(("rx2" + STEPS[step], k))
+            def _():
+                zz = dev.along("z", step)
+                sum_x(zz, step)
+                m.start(x_piece(zz, x), land["az"].at[step - 1], az.sem, z=zz)
+
+            @task(("rz2" + STEPS[step], k))
+            def _():
+                xx = dev.along("x", step)
+                sum_z(xx, step)
+                m.start(z_piece(z, xx), land["bx"].at[step - 1], bx.sem, x=xx)
+
+        if k in EAGER_OUT:
+            for step in STEPS:
+                pass_on(step)
+
         @task(("dx0", k))
         def _():
             m.wait(bufs["core"][k], cross_sem)
             add_rows(d.at[core], bufs["core"][k])
+            if k in EAGER_OUT:
+                for step in (2, 1, 3, 0):
+                    zz, xx = dev.along("z", step), dev.along("x", step)
+                    for to in STEPS:
+                        q = dev.along("x", to)
+                        m.start(x_piece(zz, q), land["ax"].at[to - 1, zz], x_sems[step], x=q)
+                    for to in STEPS:
+                        q = dev.along("z", to)
+                        m.start(z_piece(q, xx), z_land(to - 1, xx), z_sems[step], z=q)
+                return
             send(ax, "ax")
             send(bz, "bz")
 
@@ -461,12 +539,20 @@
 
         @task(("sz2", k))
         def _():
-            finish(az, "az")
+            if k in EAGER_OUT:
+                az.arrive()
+                sum_x(z, 0, *(land["az"].at[i] for i in range(3)))
+            else:
+                finish(az, "az")
             dx_ref[0:2, rows, :] = d[core, z, half, 0:2, :, cols(x)]
 
         @task(("sx2", k))
         def _():
-            finish(bx, "bx")
+            if k in EAGER_OUT:
+                bx.arrive()
+                sum_z(x, 0, *(land["bx"].at[i] for i in range(3)))
+            else:
+                finish(bx, "bx")
             dx_ref[2:4, rows, :] = d[core, z, half, 2:4, :, cols(x)]
 
     last = len(SPANS) - 1

time: 122 us -> 119 us (0.975)
  Pallas kernels: 122 us -> 119 us
    pallas_call x1, Pallas kernels: 120 us -> 117 us  [on_device(): pl.pallas_call(kernel, out_shape=(pltpu.VMEM((4, OWN, 2 * HID), BF16), pl...]
where the time goes in v5:
time: 119 us
  Pallas kernels  119 us (100%)
    pallas_call x1, Pallas kernels, on_device(): pl.pallas_call(kernel, out_shape=(pltpu.VMEM((4, OWN, 2 * HID), BF16), pl...  117 us

profile of v5, /device:TPU:1, one launch (start us, length us, event | category | flops | bytes accessed | tf_op | source)
XLA Modules:
  0.0 119.3 jit_solution(8654792304212056341)
XLA Ops:
  0.6 116.6 %shard_map.58 = (bf16[4,96,1536]{2,1,0:T(8,128)(2,1)S(1)}, bf16[4,96,384]{2,1,0:T(8,128)(2,1)S(1)}, bf16[2,768,768]{2,1,0:T(8,128)(2,1)S(1)}) custom-call(bf16[4,96,384]{2,1,0:T(8,128)(2,1)} %bitcast.10, bf16[2,2,384,768]{3,2,1,0:T(8,128)(2,1)} %bitcast.6, bf16[4,96,1536]{2,1,0:T(8,128)(2,1)} %bitcast.8), custom_call_target="tpu_custom_call" | custom-call | flops 21743271936 | bytes 8388608 | tf_op jit(solution)/shard_map/pallas_call | solution.py:568
  117.2 1.9 %shard_map.59 = (bf16[4,96,1536]{2,1,0:T(8,128)(2,1)}, bf16[4,96,384]{2,1,0:T(8,128)(2,1)}, bf16[2,2,384,768]{3,2,1,0:T(8,128)(2,1)}) custom-call(bf16[4,96,1536]{2,1,0:T(8,128)(2,1)S(1)} %get-tuple-element.9.act_ref, bf16[4,96,384]{2,1,0:T(8,128)(2,1)S(1)} %get-tuple-element.10.dx_ref, bf16[2,768,768]{2,1,0:T(8,128)(2,1)S(1)} %get-tuple-element.11.dw_ref), custom_call_target="tpu_custom_call" | custom-call | tf_op jit(solution)/shard_map/pallas_call | solution.py:615

commit v6 on v5

--- a/solution.py
+++ b/solution.py
@@ -10,7 +10,7 @@
 MESH = pl.DeviceIdType.MESH
 F32, BF16 = jnp.float32, jnp.bfloat16
 RING = 4
-STEPS = {1: "u", 3: "d", 2: "a"}
+STEPS = {2: "a", 1: "u", 3: "d"}
 SPANS = (16, 16, 16, 16, 16, 16)
 OWN = sum(SPANS)
 STARTS = tuple(sum(SPANS[:k]) for k in range(len(SPANS)))

time: 119 us -> 119 us (level)
  no operation moved by 1% of the time
where the time goes in v6:
time: 119 us
  Pallas kernels  118 us (99%)
    pallas_call x1, Pallas kernels, on_device(): pl.pallas_call(kernel, out_shape=(pltpu.VMEM((4, OWN, 2 * HID), BF16), pl...  116 us

profile of v6, /device:TPU:1, one launch (start us, length us, event | category | flops | bytes accessed | tf_op | source)
XLA Modules:
  0.0 119.2 jit_solution(17990733809984348160)
XLA Ops:
  0.6 116.4 %shard_map.58 = (bf16[4,96,1536]{2,1,0:T(8,128)(2,1)S(1)}, bf16[4,96,384]{2,1,0:T(8,128)(2,1)S(1)}, bf16[2,768,768]{2,1,0:T(8,128)(2,1)S(1)}) custom-call(bf16[4,96,384]{2,1,0:T(8,128)(2,1)} %bitcast.10, bf16[2,2,384,768]{3,2,1,0:T(8,128)(2,1)} %bitcast.6, bf16[4,96,1536]{2,1,0:T(8,128)(2,1)} %bitcast.8), custom_call_target="tpu_custom_call" | custom-call | flops 21743271936 | bytes 8388608 | tf_op jit(solution)/shard_map/pallas_call | solution.py:568
  117.1 1.9 %shard_map.59 = (bf16[4,96,1536]{2,1,0:T(8,128)(2,1)}, bf16[4,96,384]{2,1,0:T(8,128)(2,1)}, bf16[2,2,384,768]{3,2,1,0:T(8,128)(2,1)}) custom-call(bf16[4,96,1536]{2,1,0:T(8,128)(2,1)S(1)} %get-tuple-element.9.act_ref, bf16[4,96,384]{2,1,0:T(8,128)(2,1)S(1)} %get-tuple-element.10.dx_ref, bf16[2,768,768]{2,1,0:T(8,128)(2,1)S(1)} %get-tuple-element.11.dw_ref), custom_call_target="tpu_custom_call" | custom-call | tf_op jit(solution)/shard_map/pallas_call | solution.py:615
